TPU v7x, 256 devices: a whole 4x4x8 slice. The times are simulated.
256 devices in a mesh: grp: 16 (over z_hi, y, core), dev: 16 (over z_lo, x).
Axes of the slice: x: 4, y: 4, z: 8 (z_hi: 2, z_lo: 4; z = z_hi * 4 + z_lo), core: 2. Of those that a mesh axis runs over, the one named last changes fastest.
Arguments:
- inputs: bfloat16 [1024, 32, 32, 128], P(('grp', 'dev')), may hold values from -6 to 6
- cotangent: bfloat16 [1024, 32, 32, 128], P(('grp', 'dev')), may hold values from -0.09375 to 0.09375
- weights: bfloat16 [2, 1152, 128], replicated, may hold values from -0.1875 to 0.1875
- master: float32 [2, 1152, 128], P(None, 'dev'), may hold values from -0.1875 to 0.1875
- first_moment: float32 [2, 1152, 128], P(None, 'dev'), may hold values from -2 to 2
- second_moment: float32 [2, 1152, 128], P(None, 'dev'), may hold values from 0.1 to 1
Outputs:
- new_weights: bfloat16 [2, 1152, 128], replicated
- new_master: float32 [2, 1152, 128], P(None, 'dev')
- new_first: float32 [2, 1152, 128], P(None, 'dev')
- new_second: float32 [2, 1152, 128], P(None, 'dev')
All inputs are finite; a program needn't handle non-finite values.
Results may differ from a plain program's by a relative error of at most 0.0034.
Values may be sent and summed in bfloat16 or wider, within the bound.
A program may use at most 128 MiB of HBM per device.

v0:
```python
import jax
import jax.numpy as jnp
from jax import lax
from jax.sharding import PartitionSpec as P

STEP = 10


def patches(feat):
    height, width = (feat.shape[1], feat.shape[2])
    padded = jnp.pad(feat, ((0, 0), (1, 1), (1, 1), (0, 0)))
    taps = [padded[:, ti : ti + height, tj : tj + width, :] for ti in range(3) for tj in range(3)]
    return jnp.concatenate(taps, axis=-1).reshape(-1, 9 * feat.shape[3])


def flipped_kernel(kernel):
    chans = kernel.shape[1]
    blocks = kernel.reshape(9, chans, chans)[::-1]
    return blocks.transpose(0, 2, 1).reshape(9 * chans, chans)


def adamw(grad, master_part, first_part, second_part):
    first_new = 0.9 * first_part + 0.1 * grad
    second_new = 0.95 * second_part + 0.05 * grad * grad
    corr_one = 1.0 - 0.9**STEP
    corr_two = 1.0 - 0.95**STEP
    update = first_new / corr_one / (jnp.sqrt(second_new / corr_two) + 1e-08)
    master_new = master_part - 0.001 * (update + 0.1 * master_part)
    return (master_new, first_new, second_new)


def reduce_update(grad, master_shard, first_shard, second_shard):
    shard = lax.psum_scatter(grad, "dev", scatter_dimension=0, tiled=True)
    total = lax.psum(shard, "grp")
    master_new, first_new, second_new = adamw(total, master_shard, first_shard, second_shard)
    kernel_new = lax.all_gather(master_new.astype(jnp.bfloat16), "dev", axis=0, tiled=True)
    return (kernel_new, master_new, first_new, second_new)


def shards(inputs, cotangent, weights, master, first_moment, second_moment):
    shape = inputs.shape
    rows = shape[0] * shape[1] * shape[2]
    cols_in = patches(inputs)
    pre = jnp.dot(cols_in, weights[0], preferred_element_type=jnp.float32)
    act = jax.nn.silu(pre).astype(jnp.bfloat16)
    cols_act = patches(act.reshape(shape))
    cot_rows = cotangent.reshape(rows, shape[3])
    grad_second = lax.dot_general(
        cols_act, cot_rows, (((0,), (0,)), ((), ())), preferred_element_type=jnp.float32
    )
    second_layer = reduce_update(grad_second, master[1], first_moment[1], second_moment[1])
    cols_cot = patches(cotangent)
    back = jnp.dot(cols_cot, flipped_kernel(weights[1]), preferred_element_type=jnp.float32)
    sig = jax.nn.sigmoid(pre)
    dpre = (back * sig * (1.0 + pre * (1.0 - sig))).astype(jnp.bfloat16)
    grad_first = lax.dot_general(
        cols_in, dpre, (((0,), (0,)), ((), ())), preferred_element_type=jnp.float32
    )
    first_layer = reduce_update(grad_first, master[0], first_moment[0], second_moment[0])
    results = [jnp.stack([first_layer[index], second_layer[index]]) for index in range(4)]
    return (results[0], results[1], results[2], results[3])


def solution(mesh):
    placed = (
        P(("grp", "dev"), None, None, None),
        P(("grp", "dev"), None, None, None),
        P(),
        P(None, "dev", None),
        P(None, "dev", None),
        P(None, "dev", None),
    )
    return jax.shard_map(
        shards,
        mesh=mesh,
        in_specs=placed,
        out_specs=(P(), P(None, "dev", None), P(None, "dev", None), P(None, "dev", None)),
        check_vma=False,
    )
```

profile of v0, /device:TPU:2, one launch (start us, length us, event | category | flops | bytes accessed | tf_op | source)
XLA Modules:
  0.0 457.9 jit_solution(5551223594374118552)
XLA Ops:
  7.2 0.0 copy-start
  7.2 0.0 copy-start.2
  7.2 0.0 reduce-scatter.11.cloned.1.call-start
  7.2 1.7 fusion.2
  8.9 1.5 fusion.3
  10.4 1.8 fusion.4
  12.2 1.8 fusion.5
  14.0 1.5 constant_dynamic-update-slice_fusion
  15.5 0.0 copy-done
  15.5 0.7 fusion.6
  16.2 0.6 fusion.7
  16.8 0.3 fusion.8
  17.0 0.6 fusion.9
  17.7 0.0 copy-start.4
  17.7 0.0 copy-done.2
  17.7 4.3 multiply_convert_fusion
  22.0 0.0 copy-done.4
  22.0 0.0 copy-start.1
  22.0 0.3 fusion.18
  22.4 0.3 fusion.19
  22.7 0.6 fusion.20
  23.3 0.6 fusion.21
  23.8 0.3 constant_dynamic-update-slice_fusion.2
  24.1 0.7 fusion.22
  24.8 0.6 fusion.23
  25.3 0.3 fusion.24
  25.6 0.6 fusion.25
  26.2 0.0 copy-done.1
  26.3 3.7 convolution_bitcast_fusion
  29.9 0.0 reduce-scatter.11.cloned.1.call-update
  30.0 0.0 slice-start
  30.0 0.0 reduce-scatter.9.cloned.1.call-start
  30.0 0.3 fusion.10
  30.4 0.3 fusion.11
  30.7 0.6 fusion.12
  31.3 0.5 fusion.13
  31.8 0.3 constant_dynamic-update-slice_fusion.1
  32.1 0.7 fusion.14
  32.8 0.6 fusion.15
  33.3 0.3 fusion.16
  33.6 0.6 fusion.17
  34.2 0.0 copy-start.3
  34.3 3.6 copy-done.3
  37.9 0.0 slice-done
  37.9 0.2 copy.11
  38.1 0.0 copy-start.5
  38.2 0.0 copy-start.6
  38.2 0.0 copy-start.7
  38.2 17.6 %fusion.41 = f32[1152,128]{1,0:T(8,128)} fusion(bf16[4096,1152]{1,0:T(8,128)(2,1)} %bitcast.109, bf16[4096,1152]{1,0:T(8,128)(2,1)} %bitcast.107, bf16[1152,128]{1,0:T(8,128)(2,1)S(1)} %bitcast.104, f32[4096,128]{1,0:T(8,128)} %get-tuple-element.17), kind=kOutput, calls=%fused_computation.85 | convolution fusion | flops 2420637696 | bytes 21856256 | tf_op jit(solution)/shard_map/dot_general | solution.py:56
  55.7 0.0 reduce-scatter.9.cloned.1.call-update
  55.8 0.0 all-reduce.8.cloned.1.call-start
  55.8 57.4 %reduce-scatter.11.cloned.1.call-done = f32[72,128]{1,0:T(8,128)} async-done(((f32[1152,128]{1,0:T(8,128)}), f32[72,128]{1,0:T(8,128)}) %reduce-scatter.11.cloned.1.call-update) | async-done | bytes 36880
  113.2 83.3 %reduce-scatter.9.cloned.1.call-done = f32[72,128]{1,0:T(8,128)} async-done(((f32[1152,128]{1,0:T(8,128)}), f32[72,128]{1,0:T(8,128)}) %reduce-scatter.9.cloned.1.call-update) | async-done | bytes 36880
  196.6 0.0 all-reduce.8.cloned.1.call-update
  196.6 169.0 %all-reduce.8.cloned.1.call-done = (f32[72,128]{1,0:T(8,128)}, f32[72,128]{1,0:T(8,128)}) async-done(((f32[72,128]{1,0:T(8,128)}, f32[72,128]{1,0:T(8,128)}), (f32[72,128]{1,0:T(8,128)}, f32[72,128]{1,0:T(8,128)})) %all-reduce.8.cloned.1.call-update) | async-done | bytes 73744 | tf_op jit(solution)/shard_map/psum | solution.py:34
  365.6 0.0 copy-done.5
  365.6 0.0 copy-done.6
  365.6 0.0 copy-done.7
  365.6 0.9 fusion.39
  366.5 39.6 %all_gather.7 = bf16[1152,128]{1,0:T(8,128)(2,1)S(1)} all-gather(bf16[72,128]{1,0:T(8,128)(2,1)S(1)} %get-tuple-element.10), channel_id=1, replica_groups=mesh['grp'=16,'dev'=16] {'dev'}, dimensions={0}, use_global_device_ids=true | all-gather | bytes 313344 | tf_op jit(solution)/shard_map/all_gather | solution.py:36
  406.0 43.2 %all_gather.6 = bf16[1152,128]{1,0:T(8,128)(2,1)S(1)} all-gather(bf16[72,128]{1,0:T(8,128)(2,1)S(1)} %get-tuple-element.6), channel_id=1, replica_groups=mesh['grp'=16,'dev'=16] {'dev'}, dimensions={0}, use_global_device_ids=true | all-gather | bytes 313344 | tf_op jit(solution)/shard_map/all_gather | solution.py:36
  449.2 0.6 pad_maximum_fusion.1
  449.8 0.9 pad_maximum_fusion
  450.7 0.7 pad_maximum_fusion.2
  (1 shorter events, 0.0 us)
Async XLA Ops:
  7.2 8.4 %copy-start = (bf16[4,32,32,128]{3,2,1,0:T(8,128)(2,1)S(1)}, bf16[4,32,32,128]{3,2,1,0:T(8,128)(2,1)}, u32[]{:S(2)}) copy-start(bf16[4,32,32,128]{3,2,1,0:T(8,128)(2,1)} %param.6) | copy-start | bytes 3145732
  7.2 10.5 %copy-start.2 = (bf16[2,1152,128]{2,1,0:T(8,128)(2,1)S(1)}, bf16[2,1152,128]{2,1,0:T(8,128)(2,1)}, u32[]{:S(2)}) copy-start(bf16[2,1152,128]{2,1,0:T(8,128)(2,1)} %param.8) | copy-start | bytes 1769476
  7.2 106.0 %reduce-scatter.11.cloned.1.call-start = ((), (), s32[]{:S(2)}) async-start(), calls=%async_computation.3 | async-start | bytes 626688
  17.7 4.4 copy-start.4
  22.0 4.2 copy-start.1
  30.0 7.9 %slice-start = ((bf16[2,1152,128]{2,1,0:T(8,128)(2,1)}), bf16[1,1152,128]{2,1,0:T(8,128)(2,1)S(1)}, s32[]{:S(2)}) async-start(bf16[2,1152,128]{2,1,0:T(8,128)(2,1)} %param.8), calls=%async_computation.5 | async-start | bytes 589824 | tf_op jit(solution)/shard_map/slice | solution.py:53
  30.0 166.6 %reduce-scatter.9.cloned.1.call-start = ((), (), s32[]{:S(2)}) async-start(), calls=%async_computation.2 | async-start | bytes 626688
  34.2 3.7 copy-start.3
  38.1 327.4 %copy-start.5 = (f32[2,72,128]{2,1,0:T(8,128)S(1)}, f32[2,72,128]{2,1,0:T(8,128)}, u32[]{:S(2)}) copy-start(f32[2,72,128]{2,1,0:T(8,128)} %param.11) | copy-start | bytes 221188
  38.2 327.4 %copy-start.6 = (f32[2,72,128]{2,1,0:T(8,128)S(1)}, f32[2,72,128]{2,1,0:T(8,128)}, u32[]{:S(2)}) copy-start(f32[2,72,128]{2,1,0:T(8,128)} %param.10) | copy-start | bytes 221188
  38.2 327.4 %copy-start.7 = (f32[2,72,128]{2,1,0:T(8,128)S(1)}, f32[2,72,128]{2,1,0:T(8,128)}, u32[]{:S(2)}) copy-start(f32[2,72,128]{2,1,0:T(8,128)} %param.9) | copy-start | bytes 221188
  55.8 309.8 %all-reduce.8.cloned.1.call-start = ((), (), s32[]{:S(2)}) async-start(), calls=%async_computation.4 | async-start | bytes 147456 | tf_op jit(solution)/shard_map/psum | solution.py:34
Sparse Core Ops, SparseCore 0:
  30.1 83.0 reduce-scatter.10
  115.9 80.6 reduce-scatter.8
  199.3 166.2 all-reduce.7
where the time goes:
time: 458 us
  waiting for transfers between devices  310 us (68%)
  blocking collectives  82.7 us (18%)
  matrix products  25.6 us (6%)
  local copies, waits for them, and re-layouts  22.6 us (5%)
  between operations  14 us (3%)
    psum x1, waiting for transfers between devices, reduce_update(): total = lax.psum(shard, 'grp')  169 us
    unnamed x5, waiting for transfers between devices  141 us
    all_gather x2, blocking collectives, reduce_update(): lax.all_gather(master_new.astype(jnp.bfloat16), 'dev', axis=0, tiled=True)  82.7 us
    unnamed x40, local copies, waits for them, and re-layouts  20.5 us
    dot_general x1, matrix products, shards(): lax.dot_general(cols_in, dpre, (((0,), (0,)), ((), ())), preferred_elemen...  17.6 us
  transfers between devices with their start and end apart: 3, of which 3 were waited for; matrix products, arithmetic and copies ran while one was open for 5% of the time, Pallas kernels for 0%

commit v1 on v0

--- a/solution.py
+++ b/solution.py
@@ -1,9 +1,15 @@
 import jax
 import jax.numpy as jnp
 from jax import lax
+from jax.experimental import pallas as pl
+from jax.experimental.pallas import tpu as pltpu
 from jax.sharding import PartitionSpec as P
 
 STEP = 10
+MESH = pl.DeviceIdType.MESH
+N_DEV = 16
+ROWS = 72
+SLAB = 80
 
 
 def patches(feat):
@@ -29,12 +35,144 @@
     return (master_new, first_new, second_new)
 
 
-def reduce_update(grad, master_shard, first_shard, second_shard):
-    shard = lax.psum_scatter(grad, "dev", scatter_dimension=0, tiled=True)
-    total = lax.psum(shard, "grp")
-    master_new, first_new, second_new = adamw(total, master_shard, first_shard, second_shard)
-    kernel_new = lax.all_gather(master_new.astype(jnp.bfloat16), "dev", axis=0, tiled=True)
-    return (kernel_new, master_new, first_new, second_new)
+def comm_kernel(grad_ref, master_ref, first_ref, second_ref,
+                weights_ref, master_out, first_out, second_out,
+                pair_recv, dev_send, dev_recv, own_sum, col_buf, col_sum, hi_recv, total, other, gathered,
+                pair_ss, pair_rs, dev_ss, dev_rs, col_ss, col_rs, hi_ss, hi_rs, tot_ss, tot_rs,
+                gat_ss, gat_rs, fwd_ss, fwd_rs):
+    grp = lax.axis_index("grp")
+    dev = lax.axis_index("dev")
+    core = lax.rem(grp, 2)
+    col = lax.rem(grp, 8) // 2
+    high = grp // 8
+    partner = (grp + 1 - 2 * core, dev)
+    opposite = (lax.rem(grp + 8, 16), dev)
+
+    def dev_peer(step):
+        return (grp, lax.rem(dev + step, N_DEV))
+
+    def col_peer(step):
+        return (high * 8 + lax.rem(col + step, 4) * 2 + core, dev)
+
+    def remote(src, dst, ss, rs, target):
+        return pltpu.make_async_remote_copy(
+            src_ref=src, dst_ref=dst, send_sem=ss, recv_sem=rs, device_id=target, device_id_type=MESH
+        )
+
+    barrier = pltpu.get_barrier_semaphore()
+    peers = [partner, opposite] + [dev_peer(k) for k in range(1, N_DEV)] + [col_peer(k) for k in range(1, 4)]
+    for peer in peers:
+        pl.semaphore_signal(barrier, inc=1, device_id=peer, device_id_type=MESH)
+    pl.semaphore_wait(barrier, len(peers))
+
+    def shard_rows(step):
+        start = lax.rem(dev + step, N_DEV) * ROWS
+        return pl.ds(pl.multiple_of(start, 8), ROWS)
+
+    order = list(range(1, N_DEV)) + [0]
+    pair = {}
+    for k in order:
+        pair[k] = remote(grad_ref.at[1 - core, shard_rows(k), :], pair_recv.at[k], pair_ss.at[k], pair_rs.at[k], partner)
+        pair[k].start()
+    sends = []
+    for k in order:
+        pair[k].wait_recv()
+        summed = grad_ref[core, shard_rows(k), :] + pair_recv[k]
+        if k == 0:
+            own_sum[...] = summed
+        else:
+            dev_send[k, 0:ROWS, :] = summed.astype(jnp.bfloat16)
+            copy = remote(dev_send.at[k], dev_recv.at[k], dev_ss.at[k], dev_rs.at[k], dev_peer(k))
+            copy.start()
+            sends.append(copy)
+    acc = own_sum[...]
+    for copy, k in zip(sends, range(1, N_DEV)):
+        copy.wait_recv()
+        acc = acc + dev_recv[k, 0:ROWS, :].astype(jnp.float32)
+    col_buf[col] = acc
+    cols = []
+    for k in range(1, 4):
+        copy = remote(col_buf.at[col], col_buf.at[col], col_ss.at[k], col_rs.at[k], col_peer(k))
+        copy.start()
+        cols.append(copy)
+    for k in range(1, 4):
+        source = lax.rem(col + 4 - k, 4)
+        remote(col_buf.at[source], col_buf.at[source], col_ss.at[k], col_rs.at[k], col_peer(k)).wait_recv()
+    for copy in cols:
+        copy.wait_send()
+    col_sum[...] = (col_buf[0] + col_buf[1]) + (col_buf[2] + col_buf[3])
+    hi = remote(col_sum, hi_recv, hi_ss, hi_rs, opposite)
+    hi.start()
+    hi.wait_recv()
+    total[...] = col_sum[...] + hi_recv[...]
+    tot = remote(total, other, tot_ss, tot_rs, partner)
+    tot.start()
+    master_new, first_new, second_new = adamw(total[...], master_ref[core], first_ref[core], second_ref[core])
+    gathered[core, dev, 0:ROWS, :] = master_new.astype(jnp.bfloat16)
+    mine = gathered.at[core, dev]
+    gats = []
+    for k in range(1, N_DEV):
+        copy = remote(mine, mine, gat_ss.at[k], gat_rs.at[k], dev_peer(k))
+        copy.start()
+        gats.append(copy)
+    fwds = [remote(mine, mine, fwd_ss.at[0], fwd_rs.at[0], partner)]
+    fwds[0].start()
+    master_out[core] = master_new
+    first_out[core] = first_new
+    second_out[core] = second_new
+    tot.wait_recv()
+    other_new = adamw(other[...], master_ref[1 - core], first_ref[1 - core], second_ref[1 - core])
+    master_out[1 - core] = other_new[0]
+    first_out[1 - core] = other_new[1]
+    second_out[1 - core] = other_new[2]
+    for k in range(1, N_DEV):
+        source = lax.rem(dev + N_DEV - k, N_DEV)
+        slot = gathered.at[core, source]
+        remote(slot, slot, gat_ss.at[k], gat_rs.at[k], dev_peer(k)).wait_recv()
+        fwd = remote(slot, slot, fwd_ss.at[k], fwd_rs.at[k], partner)
+        fwd.start()
+        fwds.append(fwd)
+    for k in range(N_DEV):
+        source = lax.rem(dev + N_DEV - k, N_DEV)
+        slot = gathered.at[1 - core, source]
+        remote(slot, slot, fwd_ss.at[k], fwd_rs.at[k], partner).wait_recv()
+    for layer in range(2):
+        for two in range(N_DEV // 2):
+            even = gathered[layer, 2 * two, 0:ROWS, :].astype(jnp.float32)
+            odd = gathered[layer, 2 * two + 1, 0:ROWS, :].astype(jnp.float32)
+            both = jnp.concatenate([even, odd], axis=0).astype(jnp.bfloat16)
+            weights_ref[layer, 2 * ROWS * two : 2 * ROWS * (two + 1), :] = both
+    for copy in [pair[k] for k in order] + sends + gats + fwds + [hi, tot]:
+        copy.wait_send()
+
+
+def reduce_update(grads, master, first_moment, second_moment):
+    whole = pl.BlockSpec(memory_space=pltpu.VMEM)
+    state = jax.ShapeDtypeStruct(master.shape, jnp.float32)
+    dma = pltpu.SemaphoreType.DMA
+    return pl.pallas_call(
+        comm_kernel,
+        out_shape=(jax.ShapeDtypeStruct(grads.shape, jnp.bfloat16), state, state, state),
+        in_specs=[whole] * 4,
+        out_specs=(whole,) * 4,
+        scratch_shapes=[
+            pltpu.VMEM((N_DEV, ROWS, 128), jnp.float32),
+            pltpu.VMEM((N_DEV, SLAB, 128), jnp.bfloat16),
+            pltpu.VMEM((N_DEV, SLAB, 128), jnp.bfloat16),
+            pltpu.VMEM((ROWS, 128), jnp.float32),
+            pltpu.VMEM((4, ROWS, 128), jnp.float32),
+            pltpu.VMEM((ROWS, 128), jnp.float32),
+            pltpu.VMEM((ROWS, 128), jnp.float32),
+            pltpu.VMEM((ROWS, 128), jnp.float32),
+            pltpu.VMEM((ROWS, 128), jnp.float32),
+            pltpu.VMEM((2, N_DEV, SLAB, 128), jnp.bfloat16),
+            dma((N_DEV,)), dma((N_DEV,)), dma((N_DEV,)), dma((N_DEV,)),
+            dma((4,)), dma((4,)), dma, dma, dma, dma,
+            dma((N_DEV,)), dma((N_DEV,)), dma((N_DEV,)), dma((N_DEV,)),
+        ],
+        compiler_params=pltpu.CompilerParams(collective_id=0, has_side_effects=True, vmem_limit_bytes=32 * 2**20),
+        name="reduce_update",
+    )(grads, master, first_moment, second_moment)
 
 
 def shards(inputs, cotangent, weights, master, first_moment, second_moment):
@@ -48,7 +186,6 @@
     grad_second = lax.dot_general(
         cols_act, cot_rows, (((0,), (0,)), ((), ())), preferred_element_type=jnp.float32
     )
-    second_layer = reduce_update(grad_second, master[1], first_moment[1], second_moment[1])
     cols_cot = patches(cotangent)
     back = jnp.dot(cols_cot, flipped_kernel(weights[1]), preferred_element_type=jnp.float32)
     sig = jax.nn.sigmoid(pre)
@@ -56,9 +193,8 @@
     grad_first = lax.dot_general(
         cols_in, dpre, (((0,), (0,)), ((), ())), preferred_element_type=jnp.float32
     )
-    first_layer = reduce_update(grad_first, master[0], first_moment[0], second_moment[0])
-    results = [jnp.stack([first_layer[index], second_layer[index]]) for index in range(4)]
-    return (results[0], results[1], results[2], results[3])
+    grads = jnp.stack([grad_first, grad_second])
+    return reduce_update(grads, master, first_moment, second_moment)
 
 
 def solution(mesh):

time: 458 us -> 90.6 us (0.20)
  the two profiles are of different devices: /device:TPU:2 before, /device:TPU:1 now
where the time goes in v1:
time: 90.6 us; the launch traced here: 90.3 us
  Pallas kernels  39.9 us (44%)
  local copies, waits for them, and re-layouts  25.3 us (28%)
  matrix products  24.1 us (27%)
  between operations  0.91 us (1%)
    pallas_call x1, Pallas kernels, reduce_update(): pl.pallas_call(comm_kernel, out_shape=(jax.ShapeDtypeStruct(grads.shape,...  39.9 us
    unnamed x44, local copies, waits for them, and re-layouts  23.2 us
    dot_general x1, matrix products, shards(): lax.dot_general(cols_in, dpre, (((0,), (0,)), ((), ())), preferred_elemen...  16.9 us
    dot_general x1, matrix products, shards(): pre = jnp.dot(cols_in, weights[0], preferred_element_type=jnp.float32)  4.33 us
    dot_general x1, matrix products, shards(): lax.dot_general(cols_act, cot_rows, (((0,), (0,)), ((), ())), preferred_e...  2.87 us
    concatenate x3, local copies, waits for them, and re-layouts, patches(): return jnp.concatenate(taps, axis=-1).reshape(-1, 9 * feat.shape[3])  1.87 us

profile of v1, /device:TPU:1, one launch (start us, length us, event | category | flops | bytes accessed | tf_op | source)
XLA Modules:
  0.0 90.3 jit_solution(13234009025657142636)
XLA Ops:
  0.6 0.0 copy-start.3
  0.6 0.0 copy-start.5
  0.7 1.7 %fusion.2 = bf16[4,32,32,1152]{3,2,1,0:T(8,128)(2,1)S(1)} fusion(bf16[4,32,32,128]{3,2,1,0:T(8,128)(2,1)} %param.6), kind=kLoop, calls=%fused_computation.32 | loop fusion | bytes 2097152
  2.3 1.5 %fusion.3 = bf16[4,32,32,1152]{3,2,1,0:T(8,128)(2,1)S(1)} fusion(bf16[4,32,32,1152]{3,2,1,0:T(8,128)(2,1)S(1)} %fusion.2, bf16[4,32,32,128]{3,2,1,0:T(8,128)(2,1)} %param.6), kind=kLoop, calls=%fused_computation.33 | loop fusion | bytes 2097152
  3.8 1.8 %fusion.4 = bf16[4,32,32,1152]{3,2,1,0:T(8,128)(2,1)S(1)} fusion(bf16[4,32,32,1152]{3,2,1,0:T(8,128)(2,1)S(1)} %fusion.3, bf16[4,32,32,128]{3,2,1,0:T(8,128)(2,1)} %param.6), kind=kLoop, calls=%fused_computation.34 | loop fusion | bytes 2097152
  5.7 1.8 %fusion.5 = bf16[4,32,32,1152]{3,2,1,0:T(8,128)(2,1)S(1)} fusion(bf16[4,32,32,1152]{3,2,1,0:T(8,128)(2,1)S(1)} %fusion.4, bf16[4,32,32,128]{3,2,1,0:T(8,128)(2,1)} %param.6), kind=kLoop, calls=%fused_computation.35 | loop fusion | bytes 2097152
  7.5 1.5 %constant_dynamic-update-slice_fusion = bf16[4,32,32,1152]{3,2,1,0:T(8,128)(2,1)S(1)} fusion(bf16[4,32,32,1152]{3,2,1,0:T(8,128)(2,1)S(1)} %fusion.5, bf16[4,32,32,128]{3,2,1,0:T(8,128)(2,1)} %param.6), kind=kLoop, calls=%fused_computation.60 | loop fusion | bytes 2097152
  9.0 0.0 copy-done.3
  9.0 0.7 fusion.6
  9.6 0.6 fusion.7
  10.2 0.3 fusion.8
  10.5 0.6 fusion.9
  11.1 0.0 copy-start.6
  11.1 0.0 copy-done.5
  11.1 4.3 %multiply_convert_fusion = (bf16[4096,128]{1,0:T(8,128)(2,1)S(1)}, f32[4096,128]{1,0:T(8,128)}) fusion(bf16[4096,1152]{1,0:T(8,128)(2,1)S(1)} %bitcast.37, bf16[2,1152,128]{2,1,0:T(8,128)(2,1)S(1)} %copy-done.5), kind=kOutput, calls=%fused_computation.5 | convolution fusion | flops 1210580992 | bytes 12877824 | tf_op jit(solution)/shard_map/dot_general | solution.py:182
  15.4 0.0 copy-done.6
  15.4 0.0 copy-start.4
  15.4 0.3 fusion.18
  15.8 0.3 fusion.19
  16.1 0.6 fusion.20
  16.7 0.6 fusion.21
  17.3 0.3 constant_dynamic-update-slice_fusion.2
  17.5 0.7 fusion.22
  18.2 0.6 fusion.23
  18.8 0.3 fusion.24
  19.0 0.6 fusion.25
  19.6 0.0 copy-done.4
  19.7 2.9 %convolution_bitcast_fusion = f32[1,1152,128]{2,1,0:T(8,128)S(1)} fusion(bf16[4,32,32,1152]{3,2,1,0:T(8,128)(2,1)S(1)} %fusion.25, bf16[4,32,32,128]{3,2,1,0:T(8,128)(2,1)S(1)} %copy-done.4), kind=kOutput, calls=%fused_computation.3 | convolution fusion | flops 1207959552 | bytes 11075584 | tf_op jit(solution)/shard_map/dot_general | solution.py:186
  22.5 0.0 slice-start
  22.5 0.3 fusion.10
  22.9 0.3 fusion.11
  23.2 0.6 fusion.12
  23.8 0.6 fusion.13
  24.4 0.3 constant_dynamic-update-slice_fusion.1
  24.6 0.7 fusion.14
  25.3 0.6 fusion.15
  25.9 0.3 fusion.16
  26.1 0.6 fusion.17
  26.7 0.0 copy-start.7
  26.8 3.6 %copy-done.7 = bf16[4,32,32,1152]{3,2,1,0:T(8,128)(2,1)} copy-done((bf16[4,32,32,1152]{3,2,1,0:T(8,128)(2,1)}, bf16[4,32,32,1152]{3,2,1,0:T(8,128)(2,1)S(1)}, u32[]{:S(2)}) %copy-start.7) | copy-done | bytes 9437208
  30.4 0.0 slice-done
  30.4 0.2 copy.10
  30.6 0.0 copy-start
  30.7 0.0 copy-start.1
  30.7 0.0 copy-start.2
  30.7 16.9 %convolution_bitcast_fusion.1 = f32[1,1152,128]{2,1,0:T(8,128)S(1)} fusion(bf16[4096,1152]{1,0:T(8,128)(2,1)} %bitcast.38, bf16[4096,1152]{1,0:T(8,128)(2,1)} %bitcast.39, bf16[1152,128]{1,0:T(8,128)(2,1)S(1)} %bitcast.36, f32[4096,128]{1,0:T(8,128)} %get-tuple-element.5), kind=kOutput, calls=%fused_computation.4 | convolution fusion | flops 2420637696 | bytes 21856256 | tf_op jit(solution)/shard_map/dot_general | solution.py:193
  47.6 0.1 pad_maximum_fusion.grad_ref
  47.7 0.0 copy-done
  47.7 0.0 copy-done.1
  47.7 0.0 copy-done.2
  47.7 39.9 %reduce_update.1 = (bf16[2,1152,128]{2,1,0:T(8,128)(2,1)S(1)}, f32[2,72,128]{2,1,0:T(8,128)S(1)}, f32[2,72,128]{2,1,0:T(8,128)S(1)}, f32[2,72,128]{2,1,0:T(8,128)S(1)}) custom-call(f32[2,1152,128]{2,1,0:T(8,128)S(1)} %pad_maximum_fusion.grad_ref, f32[2,72,128]{2,1,0:T(8,128)S(1)} %copy-done, f32[2,72,128]{2,1,0:T(8,128)S(1)} %copy-done.1, ...), custom_call_target="tpu_custom_call" | custom-call | tf_op jit(solution)/shard_map/reduce_update/pallas_call | solution.py:153
  87.6 0.8 copy.40
  88.4 0.6 copy.41
  89.0 0.6 copy.42
  89.7 0.6 copy.43
  (1 shorter events, 0.0 us)
Async XLA Ops:
  0.6 8.3 %copy-start.3 = (bf16[4,32,32,128]{3,2,1,0:T(8,128)(2,1)S(1)}, bf16[4,32,32,128]{3,2,1,0:T(8,128)(2,1)}, u32[]{:S(2)}) copy-start(bf16[4,32,32,128]{3,2,1,0:T(8,128)(2,1)} %param.6) | copy-start | bytes 3145732
  0.6 10.5 %copy-start.5 = (bf16[2,1152,128]{2,1,0:T(8,128)(2,1)S(1)}, bf16[2,1152,128]{2,1,0:T(8,128)(2,1)}, u32[]{:S(2)}) copy-start(bf16[2,1152,128]{2,1,0:T(8,128)(2,1)} %param.8) | copy-start | bytes 1769476
  11.1 4.4 %copy-start.6 = (bf16[4,32,32,1152]{3,2,1,0:T(8,128)(2,1)}, bf16[4,32,32,1152]{3,2,1,0:T(8,128)(2,1)S(1)}, u32[]{:S(2)}) copy-start(bf16[4,32,32,1152]{3,2,1,0:T(8,128)(2,1)S(1)} %fusion.9) | copy-start | bytes 28311556
  15.4 4.2 %copy-start.4 = (bf16[4,32,32,128]{3,2,1,0:T(8,128)(2,1)S(1)}, bf16[4,32,32,128]{3,2,1,0:T(8,128)(2,1)}, u32[]{:S(2)}) copy-start(bf16[4,32,32,128]{3,2,1,0:T(8,128)(2,1)} %param.7) | copy-start | bytes 3145732
  22.5 7.9 %slice-start = ((bf16[2,1152,128]{2,1,0:T(8,128)(2,1)}), bf16[1,1152,128]{2,1,0:T(8,128)(2,1)S(1)}, s32[]{:S(2)}) async-start(bf16[2,1152,128]{2,1,0:T(8,128)(2,1)} %param.8), calls=%async_computation | async-start | bytes 589824 | tf_op jit(solution)/shard_map/slice | solution.py:190
  26.7 3.7 %copy-start.7 = (bf16[4,32,32,1152]{3,2,1,0:T(8,128)(2,1)}, bf16[4,32,32,1152]{3,2,1,0:T(8,128)(2,1)S(1)}, u32[]{:S(2)}) copy-start(bf16[4,32,32,1152]{3,2,1,0:T(8,128)(2,1)S(1)} %fusion.17) | copy-start | bytes 28311556
  30.6 17.1 %copy-start = (f32[2,72,128]{2,1,0:T(8,128)S(1)}, f32[2,72,128]{2,1,0:T(8,128)}, u32[]{:S(2)}) copy-start(f32[2,72,128]{2,1,0:T(8,128)} %master_ref.1) | copy-start | bytes 221188
  30.7 17.1 %copy-start.1 = (f32[2,72,128]{2,1,0:T(8,128)S(1)}, f32[2,72,128]{2,1,0:T(8,128)}, u32[]{:S(2)}) copy-start(f32[2,72,128]{2,1,0:T(8,128)} %first_ref.1) | copy-start | bytes 221188
  30.7 17.1 %copy-start.2 = (f32[2,72,128]{2,1,0:T(8,128)S(1)}, f32[2,72,128]{2,1,0:T(8,128)}, u32[]{:S(2)}) copy-start(f32[2,72,128]{2,1,0:T(8,128)} %second_ref.1) | copy-start | bytes 221188

commit v2 on v0

v2 whole, which is shorter than its diff:
```python
import jax
import jax.numpy as jnp
from jax import lax
from jax.experimental import pallas as pl
from jax.experimental.pallas import tpu as pltpu
from jax.sharding import PartitionSpec as P

STEP = 10
MESH = pl.DeviceIdType.MESH
BF16, F32 = jnp.bfloat16, jnp.float32
BATCH, CHANS = 4, 128
ROWS = 72
SLAB = 80
PART = 9
PAD = 16


def adamw(grad, master_part, first_part, second_part):
    first_new = 0.9 * first_part + 0.1 * grad
    second_new = 0.95 * second_part + 0.05 * grad * grad
    corr_one = 1.0 - 0.9**STEP
    corr_two = 1.0 - 0.95**STEP
    update = first_new / corr_one / (jnp.sqrt(second_new / corr_two) + 1e-08)
    master_new = master_part - 0.001 * (update + 0.1 * master_part)
    return (master_new, first_new, second_new)


def swap_pairs(tiles):
    row = lax.broadcasted_iota(jnp.int32, tiles[0].shape, 1)
    low = row < 4
    half = [
        jnp.where(low, tiles[0], pltpu.roll(tiles[2], 4, 1)),
        jnp.where(low, tiles[1], pltpu.roll(tiles[3], 4, 1)),
        jnp.where(low, pltpu.roll(tiles[0], 4, 1), tiles[2]),
        jnp.where(low, pltpu.roll(tiles[1], 4, 1), tiles[3]),
    ]
    even = lax.rem(row, 4) < 2
    return [
        jnp.where(even, half[0], pltpu.roll(half[1], 2, 1)),
        jnp.where(even, pltpu.roll(half[0], 6, 1), half[1]),
        jnp.where(even, half[2], pltpu.roll(half[3], 2, 1)),
        jnp.where(even, pltpu.roll(half[2], 6, 1), half[3]),
    ]


def shift_store(src_ref, dst_ref, image):
    col = lax.broadcasted_iota(jnp.int32, (16, 32, CHANS), 1)
    for odd in range(2):
        rows = src_ref[image, :, odd]
        wide = rows.astype(F32)
        left = jnp.where(col == 0, 0.0, pltpu.roll(wide, 1, 1)).astype(BF16)
        right = jnp.where(col == 31, 0.0, pltpu.roll(wide, 31, 1)).astype(BF16)
        place = pl.ds(odd, 16)
        dst_ref[image, 1 - odd, place, :, 0:128] = left
        dst_ref[image, 1 - odd, place, :, 128:256] = rows
        dst_ref[image, 1 - odd, place, :, 256:384] = right
    zero = jnp.zeros((32, 3 * CHANS), BF16)
    dst_ref[image, 0, 0] = zero
    dst_ref[image, 1, 16] = zero


def four_rows(ref, image):
    return jnp.concatenate(
        [ref[image, k % 2, pl.ds(k // 2, 16)].reshape(512, 3 * CHANS) for k in range(4)], axis=1
    )


def pair_weights(w_ref, forward_ref, backward_ref):
    zero = jnp.zeros((CHANS, CHANS), BF16)
    for k in range(4):
        for tj in range(3):
            rows = pl.ds((k * 3 + tj) * CHANS, CHANS)
            for odd in range(2):
                cols = pl.ds(odd * CHANS, CHANS)
                if 0 <= k - odd <= 2:
                    tap = (k - odd) * 3 + tj
                    forward_ref[rows, cols] = w_ref[0, tap * CHANS : (tap + 1) * CHANS, :]
                    tap = (odd - k + 2) * 3 + 2 - tj
                    block = w_ref[1, tap * CHANS : (tap + 1) * CHANS, :]
                    backward_ref[rows, cols] = block.astype(F32).T.astype(BF16)
                else:
                    forward_ref[rows, cols] = zero
                    backward_ref[rows, cols] = zero


def outer_sum(lhs_ref, ref):
    rhs = jnp.concatenate([four_rows(ref, image) for image in range(BATCH)], axis=0)
    lhs = lhs_ref[...].reshape(BATCH * 512, 2 * CHANS)
    return lax.dot_general(lhs, rhs, (((0,), (0,)), ((), ())), preferred_element_type=F32)


def step_kernel(x_ref, c_ref, w_ref, master_ref, first_ref, second_ref,
                gathered_out, totals_out,
                x3, c3, forward_w, backward_w, act, slope, dpre, grads,
                pair_recv, xy_send, xy_recv, xy_own, sums, z_send, z_recv, part, new_part,
                w_parts, t_parts, whole_w, totals, gathered,
                pair_ss, pair_rs, xy_ss, xy_rs, z_ss, z_rs, w_ss, w_rs, t_ss, t_rs, tot_ss, tot_rs,
                gat_ss, gat_rs, fwd_ss, fwd_rs):
    grp = lax.axis_index("grp")
    dev = lax.axis_index("dev")
    core = lax.rem(grp, 2)
    y = lax.rem(grp, 8) // 2
    z_hi = grp // 8
    x = lax.rem(dev, 4)
    z_lo = dev // 4
    z = z_hi * 4 + z_lo
    partner = (grp + 1 - 2 * core, dev)

    def xy_peer(kx, ky):
        return (z_hi * 8 + lax.rem(y + ky, 4) * 2 + core, z_lo * 4 + lax.rem(x + kx, 4))

    def z_peer(kz):
        other = lax.rem(z + kz, 8)
        return (other // 4 * 8 + y * 2 + core, lax.rem(other, 4) * 4 + x)

    def z_slot(place):
        return lax.rem(place, 4) * 2 + place // 4

    def t_peer(ky, kh):
        return (lax.rem(z_hi + kh, 2) * 8 + lax.rem(y + ky, 4) * 2 + core, dev)

    def remote(src, dst, ss, rs, target):
        return pltpu.make_async_remote_copy(
            src_ref=src, dst_ref=dst, send_sem=ss, recv_sem=rs, device_id=target, device_id_type=MESH
        )

    xy_steps = [(kx, ky) for kx in (1, 2, 3, 0) for ky in (1, 2, 3, 0) if kx or ky]
    t_steps = [(ky, kh) for ky in range(4) for kh in range(2) if ky or kh]
    peers = [partner] + [xy_peer(*k) for k in xy_steps] + [z_peer(k) for k in range(1, 8)]
    peers += [t_peer(k, 1) for k in range(1, 4)]
    barrier = pltpu.get_barrier_semaphore()
    for peer in peers:
        pl.semaphore_signal(barrier, inc=1, device_id=peer, device_id_type=MESH)

    def shard_rows(kx, lo):
        start = (lo * 4 + lax.rem(x + kx, 4)) * ROWS
        return pl.ds(pl.multiple_of(start, 8), ROWS)

    def pair_copy(layer, kx, lo):
        slot = kx * 4 + lo
        return remote(grads.at[layer, shard_rows(kx, lo), :], pair_recv.at[slot], pair_ss.at[slot], pair_rs.at[slot], partner)

    def xy_copy(kx, ky):
        slot = kx * 4 + ky
        return remote(xy_send.at[kx, lax.rem(y + ky, 4)], xy_recv.at[slot], xy_ss.at[slot], xy_rs.at[slot], xy_peer(kx, ky))

    def send_pair(layer):
        for kx in (1, 2, 3, 0):
            for lo in range(4):
                pair_copy(layer, kx, lo).start()

    def sum_pair(layer):
        for kx in (1, 2, 3, 0):
            tiles = []
            for lo in range(4):
                pair_copy(layer, kx, lo).wait_recv()
                both = grads[layer, shard_rows(kx, lo), :] + pair_recv[kx * 4 + lo]
                tiles.append(both.reshape(PART, 8, CHANS))
            for ky, tile in enumerate(swap_pairs(tiles)):
                tile = tile.reshape(ROWS, CHANS)
                if kx == 0:
                    xy_own[ky] = tile
                xy_send[kx, ky, 0:ROWS, :] = tile.astype(BF16)
            for ky in (1, 2, 3, 0):
                if kx or ky:
                    xy_copy(kx, ky).start()

    pair_weights(w_ref, forward_w, backward_w)
    for image in range(BATCH):
        shift_store(x_ref, x3, image)
        pre = jnp.dot(four_rows(x3, image), forward_w[...], preferred_element_type=F32)
        sig = 1.0 / (1.0 + jnp.exp(-pre))
        act[image] = (pre * sig).astype(BF16)
        slope[image] = sig * (1.0 + pre * (1.0 - sig))
        shift_store(c_ref, c3, image)
    out = outer_sum(act, c3)
    for ti in range(3):
        for tj in range(3):
            tap = ti * 3 + tj
            parts = [out[o * 128 : (o + 1) * 128, ((o + 2 - ti) * 3 + 2 - tj) * 128 :][:, :128] for o in range(2)]
            grads[1, tap * 128 : (tap + 1) * 128, :] = parts[0] + parts[1]

    pl.semaphore_wait(barrier, len(peers))

    @pl.when(core == 0)
    def _():
        send_pair(1)

    for image in range(BATCH):
        back = jnp.dot(four_rows(c3, image), backward_w[...], preferred_element_type=F32)
        dpre[image] = (back * slope[image]).astype(BF16)

    @pl.when(core == 1)
    def _():
        sum_pair(1)

    out = outer_sum(dpre, x3)
    for ti in range(3):
        for tj in range(3):
            tap = ti * 3 + tj
            parts = [out[o * 128 : (o + 1) * 128, ((ti + o) * 3 + tj) * 128 :][:, :128] for o in range(2)]
            grads[0, tap * 128 : (tap + 1) * 128, :] = (parts[0] + parts[1]).T

    @pl.when(core == 1)
    def _():
        send_pair(0)

    @pl.when(core == 0)
    def _():
        sum_pair(0)

    acc = xy_own[y]
    for kx, ky in xy_steps:
        xy_copy(kx, ky).wait_recv()
        acc = acc + xy_recv[kx * 4 + ky, 0:ROWS, :].astype(F32)
    sums[...] = acc
    for place in range(8):
        z_send[place, 0:PART, :] = sums[pl.ds(place, PART, stride=8), :]

    def z_copy(kz):
        return remote(z_send.at[z_slot(lax.rem(z + kz, 8))], z_recv.at[kz], z_ss.at[kz], z_rs.at[kz], z_peer(kz))

    for kz in (4, 3, 5, 2, 6, 1, 7):
        z_copy(kz).start()
    mine = z_send[z_slot(z), 0:PART, :]
    for kz in (1, 7, 2, 6, 3, 5, 4):
        z_copy(kz).wait_recv()
        mine = mine + z_recv[kz, 0:PART, :]

    own = y * 2 + z_hi
    t_parts[own, 0:PART, :] = mine
    held = pl.ds(own, PART, stride=8)
    state = [ref.at[core][held, :] for ref in (master_ref, first_ref, second_ref)]
    w_parts[z_slot(z), 0:PART, :] = adamw(mine, *state)[0]

    def w_copy(kz, place):
        slot = w_parts.at[z_slot(place)]
        return remote(slot, slot, w_ss.at[kz], w_rs.at[kz], z_peer(kz))

    def t_copy(ky, kh, place):
        slot = t_parts.at[place]
        k = ky * 2 + kh
        return remote(slot, slot, t_ss.at[k], t_rs.at[k], t_peer(ky, kh))

    for kz in (4, 3, 5, 2, 6, 1, 7):
        w_copy(kz, z).start()
    for ky, kh in t_steps:
        t_copy(ky, kh, own).start()
    for kz in range(1, 8):
        w_copy(kz, lax.rem(z + 8 - kz, 8)).wait_recv()
    for place in range(8):
        whole_w[pl.ds(place, PART, stride=8), :] = w_parts[place, 0:PART, :]
    gathered[core, x * 4 + y, 0:ROWS, :] = whole_w[...].astype(BF16)

    def gat_copy(kx, ky, slot):
        return remote(slot, slot, gat_ss.at[kx * 4 + ky], gat_rs.at[kx * 4 + ky], xy_peer(kx, ky))

    def source(layer, kx, ky):
        return gathered.at[layer, lax.rem(x + 4 - kx, 4) * 4 + lax.rem(y + 4 - ky, 4)]

    def fwd_copy(layer, kx, ky):
        slot = source(layer, kx, ky)
        return remote(slot, slot, fwd_ss.at[kx * 4 + ky], fwd_rs.at[kx * 4 + ky], partner)

    for kx, ky in xy_steps:
        gat_copy(kx, ky, source(core, 0, 0)).start()
    fwd_copy(core, 0, 0).start()
    for ky, kh in t_steps:
        place = lax.rem(y + 4 - ky, 4) * 2 + lax.rem(z_hi + kh, 2)
        t_copy(ky, kh, place).wait_recv()
    for place in range(8):
        new_part[pl.ds(place, PART, stride=8), :] = t_parts[place, 0:PART, :]
    totals[core] = new_part[...]
    tot = remote(totals.at[core], totals.at[core], tot_ss, tot_rs, partner)
    tot.start()
    for kx, ky in xy_steps:
        gat_copy(kx, ky, source(core, kx, ky)).wait_recv()
        fwd_copy(core, kx, ky).start()
    remote(totals.at[1 - core], totals.at[1 - core], tot_ss, tot_rs, partner).wait_recv()
    totals_out[...] = totals[...]
    for kx, ky in xy_steps + [(0, 0)]:
        fwd_copy(1 - core, kx, ky).wait_recv()
    gathered_out[...] = gathered[...]
    for kx in range(4):
        for k in range(4):
            pair_copy(1 - core, kx, k).wait_send()
            fwd_copy(core, kx, k).wait_send()
    for kx, ky in xy_steps:
        xy_copy(kx, ky).wait_send()
        gat_copy(kx, ky, source(core, 0, 0)).wait_send()
    for kz in range(1, 8):
        z_copy(kz).wait_send()
        w_copy(kz, z).wait_send()
    for ky, kh in t_steps:
        t_copy(ky, kh, own).wait_send()
    tot.wait_send()


def finish_kernel(gathered_ref, totals_ref, master_ref, first_ref, second_ref,
                  weights_out, master_out, first_out, second_out):
    for layer in range(2):
        new = adamw(totals_ref[layer], master_ref[layer], first_ref[layer], second_ref[layer])
        for ref, value in zip((master_out, first_out, second_out), new):
            ref[layer] = value
        shards_of = {}
        for x in range(4):
            tiles = [gathered_ref[layer, x * 4 + y, 0:ROWS, :].astype(F32).reshape(PART, 8, CHANS) for y in range(4)]
            for lo, tile in enumerate(swap_pairs(tiles)):
                shards_of[lo * 4 + x] = tile.reshape(ROWS, CHANS)
        for two in range(8):
            both = jnp.concatenate([shards_of[2 * two], shards_of[2 * two + 1]], axis=0)
            weights_out[layer, 2 * ROWS * two : 2 * ROWS * (two + 1), :] = both.astype(BF16)


def shards(inputs, cotangent, weights, master, first_moment, second_moment):
    whole = pl.BlockSpec(memory_space=pltpu.VMEM)
    dma = pltpu.SemaphoreType.DMA
    vmem = pltpu.VMEM
    by_pairs = (BATCH, 16, 2, 32, CHANS)
    gathered, totals = pl.pallas_call(
        step_kernel,
        out_shape=(
            jax.ShapeDtypeStruct((2, 16, SLAB, CHANS), BF16),
            jax.ShapeDtypeStruct((2, ROWS, CHANS), F32),
        ),
        in_specs=[whole] * 6,
        out_specs=(whole, whole),
        scratch_shapes=[
            vmem((BATCH, 2, 17, 32, 3 * CHANS), BF16),
            vmem((BATCH, 2, 17, 32, 3 * CHANS), BF16),
            vmem((12 * CHANS, 2 * CHANS), BF16),
            vmem((12 * CHANS, 2 * CHANS), BF16),
            vmem((BATCH, 512, 2 * CHANS), BF16),
            vmem((BATCH, 512, 2 * CHANS), F32),
            vmem((BATCH, 512, 2 * CHANS), BF16),
            vmem((2, 9 * CHANS, CHANS), F32),
            vmem((16, ROWS, CHANS), F32),
            vmem((4, 4, SLAB, CHANS), BF16),
            vmem((16, SLAB, CHANS), BF16),
            vmem((4, ROWS, CHANS), F32),
            vmem((ROWS, CHANS), F32),
            vmem((8, PAD, CHANS), F32),
            vmem((8, PAD, CHANS), F32),
            vmem((PAD, CHANS), F32),
            vmem((ROWS, CHANS), F32),
            vmem((8, PAD, CHANS), F32),
            vmem((8, PAD, CHANS), F32),
            vmem((ROWS, CHANS), F32),
            vmem((2, ROWS, CHANS), F32),
            vmem((2, 16, SLAB, CHANS), BF16),
            dma((16,)), dma((16,)), dma((16,)), dma((16,)), dma((8,)), dma((8,)), dma((8,)), dma((8,)),
            dma((8,)), dma((8,)), dma, dma, dma((16,)), dma((16,)), dma((16,)), dma((16,)),
        ],
        compiler_params=pltpu.CompilerParams(collective_id=0, has_side_effects=True, vmem_limit_bytes=56 * 2**20),
        name="step",
    )(inputs.reshape(by_pairs), cotangent.reshape(by_pairs), weights, master, first_moment, second_moment)
    state = jax.ShapeDtypeStruct(master.shape, F32)
    return pl.pallas_call(
        finish_kernel,
        out_shape=(jax.ShapeDtypeStruct(weights.shape, BF16), state, state, state),
        in_specs=[whole] * 5,
        out_specs=(whole,) * 4,
        compiler_params=pltpu.CompilerParams(vmem_limit_bytes=16 * 2**20),
        name="finish",
    )(gathered, totals, master, first_moment, second_moment)


def solution(mesh):
    placed = (
        P(("grp", "dev"), None, None, None),
        P(("grp", "dev"), None, None, None),
        P(),
        P(None, "dev", None),
        P(None, "dev", None),
        P(None, "dev", None),
    )
    return jax.shard_map(
        shards,
        mesh=mesh,
        in_specs=placed,
        out_specs=(P(), P(None, "dev", None), P(None, "dev", None), P(None, "dev", None)),
        check_vma=False,
    )
```

time: 458 us -> 47.7 us (0.10)
  the two profiles are of different devices: /device:TPU:2 before, /device:TPU:1 now
where the time goes in v2:
time: 47.7 us; the launch traced here: 47.5 us
  Pallas kernels  44.8 us (94%)
  local copies, waits for them, and re-layouts  1.98 us (4%)
  between operations  0.7 us (1%)
    pallas_call x1, Pallas kernels, shards(): pl.pallas_call(step_kernel, out_shape=(jax.ShapeDtypeStruct((2, 16, SLAB,...  43.7 us
    unnamed x10, local copies, waits for them, and re-layouts  1.98 us
    pallas_call x1, Pallas kernels, shards(): pl.pallas_call(finish_kernel, out_shape=(jax.ShapeDtypeStruct(weights.sha...  1.15 us

profile of v2, /device:TPU:1, one launch (start us, length us, event | category | flops | bytes accessed | tf_op | source)
XLA Modules:
  0.0 47.5 jit_solution(12488719440916905059)
XLA Ops:
  0.6 0.0 copy-start.1
  0.6 0.0 copy-start.2
  0.7 0.0 copy-start.3
  0.7 43.7 %step.1 = (bf16[2,16,80,128]{3,2,1,0:T(8,128)(2,1)}, f32[2,72,128]{2,1,0:T(8,128)}) custom-call(bf16[4,16,2,32,128]{4,3,2,1,0:T(8,128)(2,1)} %bitcast.2, bf16[4,16,2,32,128]{4,3,2,1,0:T(8,128)(2,1)} %bitcast.3, bf16[2,1152,128]{2,1,0:T(8,128)(2,1)} %w_ref.1, f32[2,72,128]{2,1,0:T(8,128)} %master_ref.3, f32[2,72,128]{2,1,0:T(8,128)} %first_ref.3, ...), custom_call_target="tpu_custom_call" | custom-call | tf_op jit(solution)/shard_map/step/pallas_call | solution.py:320
  44.3 0.0 copy-done.1
  44.3 0.0 copy-done.2
  44.4 0.0 copy-done.3
  44.4 0.0 copy-start
  44.4 1.1 %copy-done = bf16[2,16,80,128]{3,2,1,0:T(8,128)(2,1)S(1)} copy-done((bf16[2,16,80,128]{3,2,1,0:T(8,128)(2,1)S(1)}, bf16[2,16,80,128]{3,2,1,0:T(8,128)(2,1)}, u32[]{:S(2)}) %copy-start) | copy-done | bytes 655384
  45.5 0.0 copy-start.4
  45.5 0.9 %copy-done.4 = f32[2,72,128]{2,1,0:T(8,128)S(1)} copy-done((f32[2,72,128]{2,1,0:T(8,128)S(1)}, f32[2,72,128]{2,1,0:T(8,128)}, u32[]{:S(2)}) %copy-start.4) | copy-done | bytes 73752
  46.3 1.1 %finish.1 = (bf16[2,1152,128]{2,1,0:T(8,128)(2,1)}, f32[2,72,128]{2,1,0:T(8,128)}, f32[2,72,128]{2,1,0:T(8,128)}, f32[2,72,128]{2,1,0:T(8,128)}) custom-call(bf16[2,16,80,128]{3,2,1,0:T(8,128)(2,1)S(1)} %copy-done, f32[2,72,128]{2,1,0:T(8,128)S(1)} %copy-done.4, f32[2,72,128]{2,1,0:T(8,128)S(1)} %copy-done.1, f32[2,72,128]{2,1,0:T(8,128)S(1)} %copy-done.2, ...), custom_call_target="tpu_custom_call" | custom-call | tf_op jit(solution)/shard_map/finish/pallas_call | solution.py:358
Async XLA Ops:
  0.6 43.7 %copy-start.1 = (f32[2,72,128]{2,1,0:T(8,128)S(1)}, f32[2,72,128]{2,1,0:T(8,128)}, u32[]{:S(2)}) copy-start(f32[2,72,128]{2,1,0:T(8,128)} %master_ref.3) | copy-start | bytes 221188
  0.6 43.7 %copy-start.2 = (f32[2,72,128]{2,1,0:T(8,128)S(1)}, f32[2,72,128]{2,1,0:T(8,128)}, u32[]{:S(2)}) copy-start(f32[2,72,128]{2,1,0:T(8,128)} %first_ref.3) | copy-start | bytes 221188
  0.7 43.7 %copy-start.3 = (f32[2,72,128]{2,1,0:T(8,128)S(1)}, f32[2,72,128]{2,1,0:T(8,128)}, u32[]{:S(2)}) copy-start(f32[2,72,128]{2,1,0:T(8,128)} %second_ref.3) | copy-start | bytes 221188
  44.4 1.1 %copy-start = (bf16[2,16,80,128]{3,2,1,0:T(8,128)(2,1)S(1)}, bf16[2,16,80,128]{3,2,1,0:T(8,128)(2,1)}, u32[]{:S(2)}) copy-start(bf16[2,16,80,128]{3,2,1,0:T(8,128)(2,1)} %get-tuple-element.6.gathered_ref) | copy-start | bytes 1966084
  45.5 0.9 %copy-start.4 = (f32[2,72,128]{2,1,0:T(8,128)S(1)}, f32[2,72,128]{2,1,0:T(8,128)}, u32[]{:S(2)}) copy-start(f32[2,72,128]{2,1,0:T(8,128)} %get-tuple-element.7.totals_ref) | copy-start | bytes 221188

commit v3 on v2

--- a/solution.py
+++ b/solution.py
@@ -89,12 +89,13 @@
     return lax.dot_general(lhs, rhs, (((0,), (0,)), ((), ())), preferred_element_type=F32)
 
 
-def step_kernel(x_ref, c_ref, w_ref, master_ref, first_ref, second_ref,
+def step_kernel(x_hbm, c_hbm, w_hbm, master_hbm, first_hbm, second_hbm,
                 gathered_out, totals_out,
+                x_ref, c_ref, w_ref, state_ref,
                 x3, c3, forward_w, backward_w, act, slope, dpre, grads,
-                pair_recv, xy_send, xy_recv, xy_own, sums, z_send, z_recv, part, new_part,
-                w_parts, t_parts, whole_w, totals, gathered,
-                pair_ss, pair_rs, xy_ss, xy_rs, z_ss, z_rs, w_ss, w_rs, t_ss, t_rs, tot_ss, tot_rs,
+                pair_recv, xy_send, xy_recv, xy_own, z_parts, sums, held, held_whole,
+                t_parts, new_part, totals, gathered,
+                load_s, pair_ss, pair_rs, xy_ss, xy_rs, z_ss, z_rs, held_ss, held_rs, t_ss, t_rs, tot_ss, tot_rs,
                 gat_ss, gat_rs, fwd_ss, fwd_rs):
     grp = lax.axis_index("grp")
     dev = lax.axis_index("dev")
@@ -113,21 +114,27 @@
         other = lax.rem(z + kz, 8)
         return (other // 4 * 8 + y * 2 + core, lax.rem(other, 4) * 4 + x)
 
-    def z_slot(place):
-        return lax.rem(place, 4) * 2 + place // 4
-
-    def t_peer(ky, kh):
-        return (lax.rem(z_hi + kh, 2) * 8 + lax.rem(y + ky, 4) * 2 + core, dev)
+    def held_peer(k):
+        return (grp, lax.rem(z_lo + k, 4) * 4 + x)
 
     def remote(src, dst, ss, rs, target):
         return pltpu.make_async_remote_copy(
             src_ref=src, dst_ref=dst, send_sem=ss, recv_sem=rs, device_id=target, device_id_type=MESH
         )
 
-    xy_steps = [(kx, ky) for kx in (1, 2, 3, 0) for ky in (1, 2, 3, 0) if kx or ky]
-    t_steps = [(ky, kh) for ky in range(4) for kh in range(2) if ky or kh]
-    peers = [partner] + [xy_peer(*k) for k in xy_steps] + [z_peer(k) for k in range(1, 8)]
-    peers += [t_peer(k, 1) for k in range(1, 4)]
+    loads = [
+        pltpu.make_async_copy(src, dst, load_s.at[k])
+        for k, (src, dst) in enumerate(
+            [(x_hbm, x_ref), (w_hbm, w_ref), (c_hbm, c_ref), (master_hbm, state_ref.at[0]),
+             (first_hbm, state_ref.at[1]), (second_hbm, state_ref.at[2])]
+        )
+    ]
+    for copy in loads:
+        copy.start()
+    xy_order = [(kx, ky) for kx in (2, 1, 3, 0) for ky in (2, 1, 3, 0) if kx or ky]
+    xy_steps = [(kx, ky) for kx in (0, 1, 3, 2) for ky in (0, 1, 3, 2) if kx or ky]
+    z_order = (4, 3, 5, 2, 6, 1, 7)
+    peers = [partner] + [xy_peer(*k) for k in xy_steps] + [z_peer(k) for k in z_order]
     barrier = pltpu.get_barrier_semaphore()
     for peer in peers:
         pl.semaphore_signal(barrier, inc=1, device_id=peer, device_id_type=MESH)
@@ -145,12 +152,12 @@
         return remote(xy_send.at[kx, lax.rem(y + ky, 4)], xy_recv.at[slot], xy_ss.at[slot], xy_rs.at[slot], xy_peer(kx, ky))
 
     def send_pair(layer):
-        for kx in (1, 2, 3, 0):
+        for kx in (2, 1, 3, 0):
             for lo in range(4):
                 pair_copy(layer, kx, lo).start()
 
     def sum_pair(layer):
-        for kx in (1, 2, 3, 0):
+        for kx in (2, 1, 3, 0):
             tiles = []
             for lo in range(4):
                 pair_copy(layer, kx, lo).wait_recv()
@@ -161,10 +168,12 @@
                 if kx == 0:
                     xy_own[ky] = tile
                 xy_send[kx, ky, 0:ROWS, :] = tile.astype(BF16)
-            for ky in (1, 2, 3, 0):
+            for ky in (2, 1, 3, 0):
                 if kx or ky:
                     xy_copy(kx, ky).start()
 
+    for copy in loads:
+        copy.wait()
     pair_weights(w_ref, forward_w, backward_w)
     for image in range(BATCH):
         shift_store(x_ref, x3, image)
@@ -182,6 +191,16 @@
 
     pl.semaphore_wait(barrier, len(peers))
 
+    for k in range(3):
+        for h in range(2):
+            held[z_lo, k, h, 0:PART, :] = state_ref.at[k, core][pl.ds(y * 2 + h, PART, stride=8), :]
+
+    def held_copy(k, place):
+        return remote(held.at[place], held.at[place], held_ss.at[k], held_rs.at[k], held_peer(k))
+
+    for k in range(1, 4):
+        held_copy(k, z_lo).start()
+
     @pl.when(core == 0)
     def _():
         send_pair(1)
@@ -209,48 +228,29 @@
     def _():
         sum_pair(0)
 
+    for k in range(1, 4):
+        held_copy(k, lax.rem(z_lo + 4 - k, 4)).wait_recv()
+    for k in range(3):
+        for lo in range(4):
+            for h in range(2):
+                held_whole[k, pl.ds(lo * 2 + h, PART, stride=8), :] = held[lo, k, h, 0:PART, :]
     acc = xy_own[y]
     for kx, ky in xy_steps:
         xy_copy(kx, ky).wait_recv()
         acc = acc + xy_recv[kx * 4 + ky, 0:ROWS, :].astype(F32)
-    sums[...] = acc
-    for place in range(8):
-        z_send[place, 0:PART, :] = sums[pl.ds(place, PART, stride=8), :]
-
-    def z_copy(kz):
-        return remote(z_send.at[z_slot(lax.rem(z + kz, 8))], z_recv.at[kz], z_ss.at[kz], z_rs.at[kz], z_peer(kz))
-
-    for kz in (4, 3, 5, 2, 6, 1, 7):
-        z_copy(kz).start()
-    mine = z_send[z_slot(z), 0:PART, :]
-    for kz in (1, 7, 2, 6, 3, 5, 4):
-        z_copy(kz).wait_recv()
-        mine = mine + z_recv[kz, 0:PART, :]
-
-    own = y * 2 + z_hi
-    t_parts[own, 0:PART, :] = mine
-    held = pl.ds(own, PART, stride=8)
-    state = [ref.at[core][held, :] for ref in (master_ref, first_ref, second_ref)]
-    w_parts[z_slot(z), 0:PART, :] = adamw(mine, *state)[0]
-
-    def w_copy(kz, place):
-        slot = w_parts.at[z_slot(place)]
-        return remote(slot, slot, w_ss.at[kz], w_rs.at[kz], z_peer(kz))
-
-    def t_copy(ky, kh, place):
-        slot = t_parts.at[place]
-        k = ky * 2 + kh
-        return remote(slot, slot, t_ss.at[k], t_rs.at[k], t_peer(ky, kh))
-
-    for kz in (4, 3, 5, 2, 6, 1, 7):
-        w_copy(kz, z).start()
-    for ky, kh in t_steps:
-        t_copy(ky, kh, own).start()
-    for kz in range(1, 8):
-        w_copy(kz, lax.rem(z + 8 - kz, 8)).wait_recv()
-    for place in range(8):
-        whole_w[pl.ds(place, PART, stride=8), :] = w_parts[place, 0:PART, :]
-    gathered[core, x * 4 + y, 0:ROWS, :] = whole_w[...].astype(BF16)
+    z_parts[z] = acc
+
+    def z_copy(kz, place):
+        return remote(z_parts.at[place], z_parts.at[place], z_ss.at[kz], z_rs.at[kz], z_peer(kz))
+
+    for kz in z_order:
+        z_copy(kz, z).start()
+    for kz in z_order[::-1]:
+        z_copy(kz, lax.rem(z + 8 - kz, 8)).wait_recv()
+    halves = [(z_parts[k] + z_parts[k + 1]) + (z_parts[k + 2] + z_parts[k + 3]) for k in (0, 4)]
+    whole = halves[0] + halves[1]
+    sums[...] = whole
+    gathered[core, x * 4 + y, 0:ROWS, :] = adamw(whole, held_whole[0], held_whole[1], held_whole[2])[0].astype(BF16)
 
     def gat_copy(kx, ky, slot):
         return remote(slot, slot, gat_ss.at[kx * 4 + ky], gat_rs.at[kx * 4 + ky], xy_peer(kx, ky))
@@ -262,14 +262,22 @@
         slot = source(layer, kx, ky)
         return remote(slot, slot, fwd_ss.at[kx * 4 + ky], fwd_rs.at[kx * 4 + ky], partner)
 
-    for kx, ky in xy_steps:
+    for kx, ky in xy_order:
         gat_copy(kx, ky, source(core, 0, 0)).start()
     fwd_copy(core, 0, 0).start()
-    for ky, kh in t_steps:
-        place = lax.rem(y + 4 - ky, 4) * 2 + lax.rem(z_hi + kh, 2)
-        t_copy(ky, kh, place).wait_recv()
-    for place in range(8):
-        new_part[pl.ds(place, PART, stride=8), :] = t_parts[place, 0:PART, :]
+
+    def t_copy(ky, place):
+        return remote(t_parts.at[place], t_parts.at[place], t_ss.at[ky], t_rs.at[ky], xy_peer(0, ky))
+
+    for h in range(2):
+        t_parts[y, h, 0:PART, :] = sums[pl.ds(z_lo * 2 + h, PART, stride=8), :]
+    for ky in (2, 1, 3):
+        t_copy(ky, y).start()
+    for ky in (1, 3, 2):
+        t_copy(ky, lax.rem(y + 4 - ky, 4)).wait_recv()
+    for place in range(4):
+        for h in range(2):
+            new_part[pl.ds(place * 2 + h, PART, stride=8), :] = t_parts[place, h, 0:PART, :]
     totals[core] = new_part[...]
     tot = remote(totals.at[core], totals.at[core], tot_ss, tot_rs, partner)
     tot.start()
@@ -288,11 +296,11 @@
     for kx, ky in xy_steps:
         xy_copy(kx, ky).wait_send()
         gat_copy(kx, ky, source(core, 0, 0)).wait_send()
-    for kz in range(1, 8):
-        z_copy(kz).wait_send()
-        w_copy(kz, z).wait_send()
-    for ky, kh in t_steps:
-        t_copy(ky, kh, own).wait_send()
+    for kz in z_order:
+        z_copy(kz, z).wait_send()
+    for k in range(1, 4):
+        held_copy(k, z_lo).wait_send()
+        t_copy(k, y).wait_send()
     tot.wait_send()
 
 
@@ -323,9 +331,13 @@
             jax.ShapeDtypeStruct((2, 16, SLAB, CHANS), BF16),
             jax.ShapeDtypeStruct((2, ROWS, CHANS), F32),
         ),
-        in_specs=[whole] * 6,
+        in_specs=[pl.BlockSpec(memory_space=pltpu.HBM)] * 6,
         out_specs=(whole, whole),
         scratch_shapes=[
+            vmem(by_pairs, BF16),
+            vmem(by_pairs, BF16),
+            vmem(weights.shape, BF16),
+            vmem((3,) + master.shape, F32),
             vmem((BATCH, 2, 17, 32, 3 * CHANS), BF16),
             vmem((BATCH, 2, 17, 32, 3 * CHANS), BF16),
             vmem((12 * CHANS, 2 * CHANS), BF16),
@@ -338,20 +350,19 @@
             vmem((4, 4, SLAB, CHANS), BF16),
             vmem((16, SLAB, CHANS), BF16),
             vmem((4, ROWS, CHANS), F32),
+            vmem((8, ROWS, CHANS), F32),
             vmem((ROWS, CHANS), F32),
-            vmem((8, PAD, CHANS), F32),
-            vmem((8, PAD, CHANS), F32),
-            vmem((PAD, CHANS), F32),
-            vmem((ROWS, CHANS), F32),
-            vmem((8, PAD, CHANS), F32),
-            vmem((8, PAD, CHANS), F32),
+            vmem((4, 3, 2, PAD, CHANS), F32),
+            vmem((3, ROWS, CHANS), F32),
+            vmem((4, 2, PAD, CHANS), F32),
             vmem((ROWS, CHANS), F32),
             vmem((2, ROWS, CHANS), F32),
             vmem((2, 16, SLAB, CHANS), BF16),
-            dma((16,)), dma((16,)), dma((16,)), dma((16,)), dma((8,)), dma((8,)), dma((8,)), dma((8,)),
-            dma((8,)), dma((8,)), dma, dma, dma((16,)), dma((16,)), dma((16,)), dma((16,)),
+            dma((6,)),
+            dma((16,)), dma((16,)), dma((16,)), dma((16,)), dma((8,)), dma((8,)), dma((4,)), dma((4,)),
+            dma((4,)), dma((4,)), dma, dma, dma((16,)), dma((16,)), dma((16,)), dma((16,)),
         ],
-        compiler_params=pltpu.CompilerParams(collective_id=0, has_side_effects=True, vmem_limit_bytes=56 * 2**20),
+        compiler_params=pltpu.CompilerParams(collective_id=0, has_side_effects=True, vmem_limit_bytes=60 * 2**20),
         name="step",
     )(inputs.reshape(by_pairs), cotangent.reshape(by_pairs), weights, master, first_moment, second_moment)
     state = jax.ShapeDtypeStruct(master.shape, F32)
@@ -360,7 +371,7 @@
         out_shape=(jax.ShapeDtypeStruct(weights.shape, BF16), state, state, state),
         in_specs=[whole] * 5,
         out_specs=(whole,) * 4,
-        compiler_params=pltpu.CompilerParams(vmem_limit_bytes=16 * 2**20),
+        compiler_params=pltpu.CompilerParams(vmem_limit_bytes=60 * 2**20),
         name="finish",
     )(gathered, totals, master, first_moment, second_moment)
 

time: 47.7 us -> 43.9 us (0.920)
  local copies, waits for them, and re-layouts: 1.98 us -> 0 us
  Pallas kernels: 44.8 us -> 43.2 us
    pallas_call x1, Pallas kernels: 43.7 us -> 40.8 us  [shards(): pl.pallas_call(step_kernel, out_shape=(jax.ShapeDtypeStruct((2, 16, SLAB,...]
    unnamed x10 -> x0, local copies, waits for them, and re-layouts: 1.98 us -> none
    pallas_call x1, Pallas kernels: 1.15 us -> 2.33 us  [shards(): pl.pallas_call(finish_kernel, out_shape=(jax.ShapeDtypeStruct(weights.sha...]
where the time goes in v3:
time: 43.9 us; the launch traced here: 43.8 us
  Pallas kernels  43.2 us (98%)
  between operations  0.64 us (1%)
    pallas_call x1, Pallas kernels, shards(): pl.pallas_call(step_kernel, out_shape=(jax.ShapeDtypeStruct((2, 16, SLAB,...  40.8 us
    pallas_call x1, Pallas kernels, shards(): pl.pallas_call(finish_kernel, out_shape=(jax.ShapeDtypeStruct(weights.sha...  2.33 us

profile of v3, /device:TPU:1, one launch (start us, length us, event | category | flops | bytes accessed | tf_op | source)
XLA Modules:
  0.0 43.8 jit_solution(8882263040443767316)
XLA Ops:
  0.6 40.8 %step.1 = (bf16[2,16,80,128]{3,2,1,0:T(8,128)(2,1)}, f32[2,72,128]{2,1,0:T(8,128)}) custom-call(bf16[4,16,2,32,128]{4,3,2,1,0:T(8,128)(2,1)} %bitcast.2, bf16[4,16,2,32,128]{4,3,2,1,0:T(8,128)(2,1)} %bitcast.3, bf16[2,1152,128]{2,1,0:T(8,128)(2,1)} %w_hbm.1, f32[2,72,128]{2,1,0:T(8,128)} %master_ref.1, f32[2,72,128]{2,1,0:T(8,128)} %first_ref.1, ...), custom_call_target="tpu_custom_call" | custom-call | tf_op jit(solution)/shard_map/step/pallas_call | solution.py:328
  41.5 2.3 %finish.1 = (bf16[2,1152,128]{2,1,0:T(8,128)(2,1)}, f32[2,72,128]{2,1,0:T(8,128)}, f32[2,72,128]{2,1,0:T(8,128)}, f32[2,72,128]{2,1,0:T(8,128)}) custom-call(bf16[2,16,80,128]{3,2,1,0:T(8,128)(2,1)} %get-tuple-element.6.gathered_ref, f32[2,72,128]{2,1,0:T(8,128)} %get-tuple-element.7.totals_ref, f32[2,72,128]{2,1,0:T(8,128)} %master_ref.1, ...), custom_call_target="tpu_custom_call" | custom-call | tf_op jit(solution)/shard_map/finish/pallas_call | solution.py:369

commit v4 on v3

v4 whole, which is shorter than its diff:
```python
import jax
import jax.numpy as jnp
from jax import lax
from jax.experimental import pallas as pl
from jax.experimental.pallas import tpu as pltpu
from jax.sharding import PartitionSpec as P

STEP = 10
MESH = pl.DeviceIdType.MESH
BF16, F32 = jnp.bfloat16, jnp.float32
BATCH, CHANS = 4, 128
ROWS = 72
SLAB = 80


def adamw(grad, master_part, first_part, second_part):
    first_new = 0.9 * first_part + 0.1 * grad
    second_new = 0.95 * second_part + 0.05 * grad * grad
    corr_one = 1.0 - 0.9**STEP
    corr_two = 1.0 - 0.95**STEP
    update = first_new / corr_one / (jnp.sqrt(second_new / corr_two) + 1e-08)
    master_new = master_part - 0.001 * (update + 0.1 * master_part)
    return (master_new, first_new, second_new)


def shift_store(src_ref, dst_ref, image):
    edge = jnp.zeros((16, 1, CHANS), BF16)
    for odd in range(2):
        rows = src_ref[image, :, odd]
        place = pl.ds(odd, 16)
        dst_ref[image, 1 - odd, place, :, 0:128] = jnp.concatenate([edge, rows[:, :31]], axis=1)
        dst_ref[image, 1 - odd, place, :, 128:256] = rows
        dst_ref[image, 1 - odd, place, :, 256:384] = jnp.concatenate([rows[:, 1:], edge], axis=1)
    zero = jnp.zeros((32, 3 * CHANS), BF16)
    dst_ref[image, 0, 0] = zero
    dst_ref[image, 1, 16] = zero


def four_rows(ref, image):
    return jnp.concatenate(
        [ref[image, k % 2, pl.ds(k // 2, 16)].reshape(512, 3 * CHANS) for k in range(4)], axis=1
    )


def pair_forward(w_ref, out_ref):
    zero = jnp.zeros((CHANS, CHANS), BF16)
    for k in range(4):
        for tj in range(3):
            rows = pl.ds((k * 3 + tj) * CHANS, CHANS)
            for odd in range(2):
                tap = (k - odd) * 3 + tj
                block = w_ref[0, tap * CHANS : (tap + 1) * CHANS, :] if 0 <= k - odd <= 2 else zero
                out_ref[rows, odd * CHANS : (odd + 1) * CHANS] = block


def pair_backward(w_ref, out_ref):
    zero = jnp.zeros((CHANS, CHANS), BF16)
    for k in range(4):
        for tj in range(3):
            rows = pl.ds((k * 3 + tj) * CHANS, CHANS)
            for odd in range(2):
                tap = (odd - k + 2) * 3 + 2 - tj
                block = w_ref[1, tap * CHANS : (tap + 1) * CHANS, :].T if 0 <= k - odd <= 2 else zero
                out_ref[rows, odd * CHANS : (odd + 1) * CHANS] = block


def put_turned(ref, value, image):
    turned = value.astype(BF16).T
    for odd in range(2):
        start = odd * BATCH * 512 + image * 512
        ref[:, start : start + 512] = turned[odd * CHANS : (odd + 1) * CHANS]


def outer_sum(turned, ref):
    out = None
    for odd in range(2):
        for image in range(BATCH):
            near = jnp.concatenate(
                [ref[image, (k + odd) % 2, pl.ds((k + odd) // 2, 16)].reshape(512, 3 * CHANS) for k in range(3)], axis=1
            )
            start = odd * BATCH * 512 + image * 512
            part = jnp.dot(turned[:, start : start + 512], near, preferred_element_type=F32)
            out = part if out is None else out + part
    return out


def step_kernel(x_hbm, c_hbm, w_hbm, master_hbm, first_hbm, second_hbm,
                weights_out, totals_out,
                x_ref, c_ref, w_ref, state_ref,
                x3, c3, forward_w, backward_w, act, slope, dpre, grads,
                pair_recv, xy_send, xy_recv, xy_own, z_parts, held, totals, gathered,
                load_s, pair_ss, pair_rs, xy_ss, xy_rs, z_ss, z_rs, held_ss, held_rs, t_ss, t_rs, tot_ss, tot_rs,
                gat_ss, gat_rs, fwd_ss, fwd_rs):
    grp = lax.axis_index("grp")
    dev = lax.axis_index("dev")
    core = lax.rem(grp, 2)
    y = lax.rem(grp, 8) // 2
    z_hi = grp // 8
    x = lax.rem(dev, 4)
    z_lo = dev // 4
    z = z_hi * 4 + z_lo
    partner = (grp + 1 - 2 * core, dev)

    def xy_peer(kx, ky):
        return (z_hi * 8 + lax.rem(y + ky, 4) * 2 + core, z_lo * 4 + lax.rem(x + kx, 4))

    def z_peer(kz):
        other = lax.rem(z + kz, 8)
        return (other // 4 * 8 + y * 2 + core, lax.rem(other, 4) * 4 + x)

    def held_peer(k):
        return (grp, lax.rem(z_lo + k, 4) * 4 + x)

    def remote(src, dst, ss, rs, target):
        return pltpu.make_async_remote_copy(
            src_ref=src, dst_ref=dst, send_sem=ss, recv_sem=rs, device_id=target, device_id_type=MESH
        )

    loads = [
        pltpu.make_async_copy(src, dst, load_s.at[k])
        for k, (src, dst) in enumerate(
            [(x_hbm, x_ref), (w_hbm, w_ref), (c_hbm, c_ref)]
            + [(ref.at[layer], state_ref.at[layer, k])
               for k, ref in enumerate((master_hbm, first_hbm, second_hbm)) for layer in range(2)]
        )
    ]
    for copy in loads:
        copy.start()
    xy_order = [(kx, ky) for kx in (2, 1, 3, 0) for ky in (2, 1, 3, 0) if kx or ky]
    xy_steps = [(kx, ky) for kx in (0, 1, 3, 2) for ky in (0, 1, 3, 2) if kx or ky]
    z_order = (4, 3, 5, 2, 6, 1, 7)
    peers = [partner] + [xy_peer(*k) for k in xy_steps] + [z_peer(k) for k in z_order]
    barrier = pltpu.get_barrier_semaphore()
    for peer in peers:
        pl.semaphore_signal(barrier, inc=1, device_id=peer, device_id_type=MESH)

    def shard_rows(kx, ky):
        start = (lax.rem(y + ky, 4) * 4 + lax.rem(x + kx, 4)) * ROWS
        return pl.ds(pl.multiple_of(start, 8), ROWS)

    def pair_copy(layer, kx, ky):
        slot = kx * 4 + ky
        return remote(grads.at[layer, shard_rows(kx, ky), :], pair_recv.at[slot], pair_ss.at[slot], pair_rs.at[slot], partner)

    def xy_copy(kx, ky):
        slot = kx * 4 + ky
        return remote(xy_send.at[slot], xy_recv.at[slot], xy_ss.at[slot], xy_rs.at[slot], xy_peer(kx, ky))

    def send_pair(layer):
        for kx, ky in xy_order + [(0, 0)]:
            pair_copy(layer, kx, ky).start()

    def sum_pair(layer):
        for kx, ky in xy_order + [(0, 0)]:
            slot = kx * 4 + ky
            pair_copy(layer, kx, ky).wait_recv()
            both = grads[layer, shard_rows(kx, ky), :] + pair_recv[slot]
            if slot:
                xy_send[slot, 0:ROWS, :] = both.astype(BF16)
                xy_copy(kx, ky).start()
            else:
                xy_own[...] = both

    for copy in loads:
        copy.wait()
    pair_forward(w_ref, forward_w)
    shift_store(x_ref, x3, 0)
    for image in range(BATCH):
        pre = jnp.dot(four_rows(x3, image), forward_w[...], preferred_element_type=F32)
        sig = 1.0 / (1.0 + jnp.exp(-pre))
        value = pre * sig
        put_turned(act, value, image)
        slope[image] = sig + value * (1.0 - sig)
        if image < BATCH - 1:
            shift_store(x_ref, x3, image + 1)
        shift_store(c_ref, c3, image)
    pair_backward(w_ref, backward_w)
    out = outer_sum(act, c3)
    for block in range(9):
        tap = 8 - block
        grads[1, tap * CHANS : (tap + 1) * CHANS, :] = out[:, block * CHANS : (block + 1) * CHANS]

    pl.semaphore_wait(barrier, len(peers))

    def held_copy(k, source_ref):
        return remote(source_ref, held, held_ss.at[k], held_rs, held_peer(k))

    @pl.when(z_lo == y)
    def _():
        held[...] = state_ref[core]
        for k in range(1, 4):
            held_copy(k, held).start()

    @pl.when(core == 0)
    def _():
        send_pair(1)

    for image in range(BATCH):
        back = jnp.dot(four_rows(c3, image), backward_w[...], preferred_element_type=F32)
        put_turned(dpre, back * slope[image], image)

    @pl.when(core == 1)
    def _():
        sum_pair(1)

    out = outer_sum(dpre, x3)
    for tap in range(9):
        grads[0, tap * CHANS : (tap + 1) * CHANS, :] = out[:, tap * CHANS : (tap + 1) * CHANS].T

    @pl.when(core == 1)
    def _():
        send_pair(0)

    @pl.when(core == 0)
    def _():
        sum_pair(0)

    @pl.when(z_lo != y)
    def _():
        held_copy(1, held).wait_recv()

    acc = xy_own[...]
    for kx, ky in xy_steps:
        xy_copy(kx, ky).wait_recv()
        acc = acc + xy_recv[kx * 4 + ky, 0:ROWS, :].astype(F32)
    z_parts[z] = acc

    def z_copy(kz, place):
        return remote(z_parts.at[place], z_parts.at[place], z_ss.at[kz], z_rs.at[kz], z_peer(kz))

    for kz in z_order:
        z_copy(kz, z).start()
    for kz in z_order[::-1]:
        z_copy(kz, lax.rem(z + 8 - kz, 8)).wait_recv()
    halves = [(z_parts[k] + z_parts[k + 1]) + (z_parts[k + 2] + z_parts[k + 3]) for k in (0, 4)]
    whole = halves[0] + halves[1]
    slab = adamw(whole, held[0], held[1], held[2])[0].astype(BF16)
    gathered[core, y * 4 + x, 0:ROWS, :] = slab

    def gat_copy(kx, ky, slot):
        return remote(slot, slot, gat_ss.at[kx * 4 + ky], gat_rs.at[kx * 4 + ky], xy_peer(kx, ky))

    def source(layer, kx, ky):
        return gathered.at[layer, lax.rem(y + 4 - ky, 4) * 4 + lax.rem(x + 4 - kx, 4)]

    def fwd_copy(layer, kx, ky):
        slot = source(layer, kx, ky)
        return remote(slot, slot, fwd_ss.at[kx * 4 + ky], fwd_rs.at[kx * 4 + ky], partner)

    for kx, ky in xy_order:
        gat_copy(kx, ky, source(core, 0, 0)).start()
    fwd_copy(core, 0, 0).start()

    def t_copy(ky):
        return remote(totals.at[core], totals.at[core], t_ss.at[ky], t_rs, xy_peer(0, ky))

    @pl.when(z_lo == y)
    def _():
        totals[core] = whole
        for ky in (2, 1, 3):
            t_copy(ky).start()

    @pl.when(z_lo != y)
    def _():
        t_copy(1).wait_recv()

    tot = remote(totals.at[core], totals.at[core], tot_ss, tot_rs, partner)
    tot.start()

    def assemble(layer):
        for two in range(8):
            both = [gathered[layer, 2 * two + k, 0:ROWS, :].astype(F32) for k in range(2)]
            weights_out[layer, 2 * ROWS * two : 2 * ROWS * (two + 1), :] = jnp.concatenate(both, axis=0).astype(BF16)

    for kx, ky in xy_steps:
        gat_copy(kx, ky, source(core, kx, ky)).wait_recv()
        fwd_copy(core, kx, ky).start()
    assemble(core)
    remote(totals.at[1 - core], totals.at[1 - core], tot_ss, tot_rs, partner).wait_recv()
    totals_out[...] = totals[...]
    for kx, ky in xy_steps + [(0, 0)]:
        fwd_copy(1 - core, kx, ky).wait_recv()
    assemble(1 - core)
    for kx in range(4):
        for k in range(4):
            pair_copy(1 - core, kx, k).wait_send()
            fwd_copy(core, kx, k).wait_send()
    for kx, ky in xy_steps:
        xy_copy(kx, ky).wait_send()
        gat_copy(kx, ky, source(core, 0, 0)).wait_send()
    for kz in z_order:
        z_copy(kz, z).wait_send()

    @pl.when(z_lo == y)
    def _():
        for k in range(1, 4):
            held_copy(k, held).wait_send()
            t_copy(k).wait_send()

    tot.wait_send()


def shards(inputs, cotangent, weights, master, first_moment, second_moment):
    whole = pl.BlockSpec(memory_space=pltpu.VMEM)
    dma = pltpu.SemaphoreType.DMA
    vmem = pltpu.VMEM
    by_pairs = (BATCH, 16, 2, 32, CHANS)
    new_weights, totals = pl.pallas_call(
        step_kernel,
        out_shape=(
            jax.ShapeDtypeStruct(weights.shape, BF16),
            jax.ShapeDtypeStruct((2, ROWS, CHANS), F32),
        ),
        in_specs=[pl.BlockSpec(memory_space=pltpu.HBM)] * 6,
        out_specs=(whole, whole),
        scratch_shapes=[
            vmem(by_pairs, BF16),
            vmem(by_pairs, BF16),
            vmem(weights.shape, BF16),
            vmem((2, 3, ROWS, CHANS), F32),
            vmem((BATCH, 2, 17, 32, 3 * CHANS), BF16),
            vmem((BATCH, 2, 17, 32, 3 * CHANS), BF16),
            vmem((12 * CHANS, 2 * CHANS), BF16),
            vmem((12 * CHANS, 2 * CHANS), BF16),
            vmem((CHANS, BATCH * 1024), BF16),
            vmem((BATCH, 512, 2 * CHANS), F32),
            vmem((CHANS, BATCH * 1024), BF16),
            vmem((2, 9 * CHANS, CHANS), F32),
            vmem((16, ROWS, CHANS), F32),
            vmem((16, SLAB, CHANS), BF16),
            vmem((16, SLAB, CHANS), BF16),
            vmem((ROWS, CHANS), F32),
            vmem((8, ROWS, CHANS), F32),
            vmem((3, ROWS, CHANS), F32),
            vmem((2, ROWS, CHANS), F32),
            vmem((2, 16, SLAB, CHANS), BF16),
            dma((9,)),
            dma((16,)), dma((16,)), dma((16,)), dma((16,)), dma((8,)), dma((8,)), dma((4,)), dma,
            dma((4,)), dma, dma, dma, dma((16,)), dma((16,)), dma((16,)), dma((16,)),
        ],
        compiler_params=pltpu.CompilerParams(collective_id=0, has_side_effects=True, vmem_limit_bytes=60 * 2**20),
        name="step",
    )(inputs.reshape(by_pairs), cotangent.reshape(by_pairs), weights, master, first_moment, second_moment)
    return (new_weights,) + adamw(totals, master, first_moment, second_moment)


def solution(mesh):
    placed = (
        P(("grp", "dev"), None, None, None),
        P(("grp", "dev"), None, None, None),
        P(),
        P(None, "dev", None),
        P(None, "dev", None),
        P(None, "dev", None),
    )
    return jax.shard_map(
        shards,
        mesh=mesh,
        in_specs=placed,
        out_specs=(P(), P(None, "dev", None), P(None, "dev", None), P(None, "dev", None)),
        check_vma=False,
    )
```

time: 43.9 us -> 45.6 us (1.039)
  Pallas kernels: 43.2 us -> 41.1 us
  local copies, waits for them, and re-layouts: 0 us -> 1.93 us
  other arithmetic: 0 us -> 1.59 us
    pallas_call x2 -> x1, Pallas kernels: 43.2 us -> 41.1 us  [shards(): pl.pallas_call(step_kernel, out_shape=(jax.ShapeDtypeStruct(weights.shape...]
    unnamed x0 -> x7, local copies, waits for them, and re-layouts: none -> 1.93 us
    sub x0 -> x1, other arithmetic: none -> 1.59 us  [adamw(): master_new = master_part - 0.001 * (update + 0.1 * master_part)]
where the time goes in v4:
time: 45.6 us; the launch traced here: 45.4 us
  Pallas kernels  41.1 us (90%)
  local copies, waits for them, and re-layouts  1.93 us (4%)
  other arithmetic  1.59 us (3%)
  between operations  0.69 us (2%)
    pallas_call x1, Pallas kernels, shards(): pl.pallas_call(step_kernel, out_shape=(jax.ShapeDtypeStruct(weights.shape...  41.1 us
    unnamed x7, local copies, waits for them, and re-layouts  1.93 us
    sub x1, other arithmetic, adamw(): master_new = master_part - 0.001 * (update + 0.1 * master_part)  1.59 us

profile of v4, /device:TPU:1, one launch (start us, length us, event | category | flops | bytes accessed | tf_op | source)
XLA Modules:
  0.0 45.4 jit_solution(7935457380342379242)
XLA Ops:
  0.6 0.0 copy-start
  0.6 0.0 copy-start.1
  0.7 0.0 copy-start.2
  0.7 41.1 %step.1 = (bf16[2,1152,128]{2,1,0:T(8,128)(2,1)}, f32[2,72,128]{2,1,0:T(8,128)}) custom-call(bf16[4,16,2,32,128]{4,3,2,1,0:T(8,128)(2,1)} %bitcast.2, bf16[4,16,2,32,128]{4,3,2,1,0:T(8,128)(2,1)} %bitcast.3, bf16[2,1152,128]{2,1,0:T(8,128)(2,1)} %w_hbm.1, f32[2,72,128]{2,1,0:T(8,128)} %master_hbm.1, f32[2,72,128]{2,1,0:T(8,128)} %first_hbm.1, ...), custom_call_target="tpu_custom_call" | custom-call | tf_op jit(solution)/shard_map/step/pallas_call | solution.py:308
  41.8 0.0 copy-done
  41.8 0.0 copy-done.1
  41.8 0.0 copy-done.2
  41.8 1.6 %multiply_subtract_fusion = (f32[2,72,128]{2,1,0:T(8,128)}, f32[2,72,128]{2,1,0:T(8,128)}, f32[2,72,128]{2,1,0:T(8,128)}) fusion(f32[2,72,128]{2,1,0:T(8,128)S(1)} %copy-done, f32[2,72,128]{2,1,0:T(8,128)} %get-tuple-element.7, f32[2,72,128]{2,1,0:T(8,128)S(1)} %copy-done.1, f32[2,72,128]{2,1,0:T(8,128)S(1)} %copy-done.2), kind=kLoop, calls=%fused_computation.2 | loop fusion | flops 276480 | bytes 516096 | tf_op jit(solution)/shard_map/sub | solution.py:22
  43.4 1.9 %copy.11 = bf16[2,1152,128]{2,1,0:T(8,128)(2,1)} copy(bf16[2,1152,128]{2,1,0:T(8,128)(2,1)} %get-tuple-element.15) | data formatting | bytes 1179648
Async XLA Ops:
  0.6 41.2 %copy-start = (f32[2,72,128]{2,1,0:T(8,128)S(1)}, f32[2,72,128]{2,1,0:T(8,128)}, u32[]{:S(2)}) copy-start(f32[2,72,128]{2,1,0:T(8,128)} %master_hbm.1) | copy-start | bytes 221188
  0.6 41.2 %copy-start.1 = (f32[2,72,128]{2,1,0:T(8,128)S(1)}, f32[2,72,128]{2,1,0:T(8,128)}, u32[]{:S(2)}) copy-start(f32[2,72,128]{2,1,0:T(8,128)} %first_hbm.1) | copy-start | bytes 221188
  0.7 41.2 %copy-start.2 = (f32[2,72,128]{2,1,0:T(8,128)S(1)}, f32[2,72,128]{2,1,0:T(8,128)}, u32[]{:S(2)}) copy-start(f32[2,72,128]{2,1,0:T(8,128)} %second_hbm.1) | copy-start | bytes 221188

commit v5 on v4

--- a/solution.py
+++ b/solution.py
@@ -85,12 +85,12 @@
 
 
 def step_kernel(x_hbm, c_hbm, w_hbm, master_hbm, first_hbm, second_hbm,
-                weights_out, totals_out,
+                gathered_out, totals_out,
                 x_ref, c_ref, w_ref, state_ref,
                 x3, c3, forward_w, backward_w, act, slope, dpre, grads,
                 pair_recv, xy_send, xy_recv, xy_own, z_parts, held, totals, gathered,
                 load_s, pair_ss, pair_rs, xy_ss, xy_rs, z_ss, z_rs, held_ss, held_rs, t_ss, t_rs, tot_ss, tot_rs,
-                gat_ss, gat_rs, fwd_ss, fwd_rs):
+                gat_ss, gat_rs, fwd_ss, fwd_rs, put_s):
     grp = lax.axis_index("grp")
     dev = lax.axis_index("dev")
     core = lax.rem(grp, 2)
@@ -174,23 +174,24 @@
         if image < BATCH - 1:
             shift_store(x_ref, x3, image + 1)
         shift_store(c_ref, c3, image)
+
+    pl.semaphore_wait(barrier, len(peers))
+
+    def held_copy(k, source_ref):
+        return remote(source_ref, held, held_ss.at[k], held_rs, held_peer(k))
+
+    @pl.when(z_lo == y)
+    def _():
+        held[...] = state_ref[core]
+        for k in range(1, 4):
+            held_copy(k, held).start()
+
     pair_backward(w_ref, backward_w)
     out = outer_sum(act, c3)
     for block in range(9):
         tap = 8 - block
         grads[1, tap * CHANS : (tap + 1) * CHANS, :] = out[:, block * CHANS : (block + 1) * CHANS]
 
-    pl.semaphore_wait(barrier, len(peers))
-
-    def held_copy(k, source_ref):
-        return remote(source_ref, held, held_ss.at[k], held_rs, held_peer(k))
-
-    @pl.when(z_lo == y)
-    def _():
-        held[...] = state_ref[core]
-        for k in range(1, 4):
-            held_copy(k, held).start()
-
     @pl.when(core == 0)
     def _():
         send_pair(1)
@@ -214,16 +215,12 @@
     @pl.when(core == 0)
     def _():
         sum_pair(0)
-
-    @pl.when(z_lo != y)
-    def _():
-        held_copy(1, held).wait_recv()
 
     acc = xy_own[...]
     for kx, ky in xy_steps:
         xy_copy(kx, ky).wait_recv()
         acc = acc + xy_recv[kx * 4 + ky, 0:ROWS, :].astype(F32)
-    z_parts[z] = acc
+    z_parts[z, 0:ROWS, :] = acc.astype(BF16)
 
     def z_copy(kz, place):
         return remote(z_parts.at[place], z_parts.at[place], z_ss.at[kz], z_rs.at[kz], z_peer(kz))
@@ -232,8 +229,13 @@
         z_copy(kz, z).start()
     for kz in z_order[::-1]:
         z_copy(kz, lax.rem(z + 8 - kz, 8)).wait_recv()
-    halves = [(z_parts[k] + z_parts[k + 1]) + (z_parts[k + 2] + z_parts[k + 3]) for k in (0, 4)]
+    z_part = [z_parts[k, 0:ROWS, :].astype(F32) for k in range(8)]
+    halves = [(z_part[k] + z_part[k + 1]) + (z_part[k + 2] + z_part[k + 3]) for k in (0, 4)]
     whole = halves[0] + halves[1]
+    @pl.when(z_lo != y)
+    def _():
+        held_copy(1, held).wait_recv()
+
     slab = adamw(whole, held[0], held[1], held[2])[0].astype(BF16)
     gathered[core, y * 4 + x, 0:ROWS, :] = slab
 
@@ -267,20 +269,20 @@
     tot = remote(totals.at[core], totals.at[core], tot_ss, tot_rs, partner)
     tot.start()
 
-    def assemble(layer):
-        for two in range(8):
-            both = [gathered[layer, 2 * two + k, 0:ROWS, :].astype(F32) for k in range(2)]
-            weights_out[layer, 2 * ROWS * two : 2 * ROWS * (two + 1), :] = jnp.concatenate(both, axis=0).astype(BF16)
+    def put(layer):
+        pairs = ((gathered.at[layer], gathered_out.at[layer]), (totals.at[layer], totals_out.at[layer]))
+        return [pltpu.make_async_copy(src, dst, put_s.at[layer, k]) for k, (src, dst) in enumerate(pairs)]
 
     for kx, ky in xy_steps:
         gat_copy(kx, ky, source(core, kx, ky)).wait_recv()
         fwd_copy(core, kx, ky).start()
-    assemble(core)
+    for copy in put(core):
+        copy.start()
     remote(totals.at[1 - core], totals.at[1 - core], tot_ss, tot_rs, partner).wait_recv()
-    totals_out[...] = totals[...]
     for kx, ky in xy_steps + [(0, 0)]:
         fwd_copy(1 - core, kx, ky).wait_recv()
-    assemble(1 - core)
+    for copy in put(1 - core):
+        copy.start()
     for kx in range(4):
         for k in range(4):
             pair_copy(1 - core, kx, k).wait_send()
@@ -298,21 +300,55 @@
             t_copy(k).wait_send()
 
     tot.wait_send()
+    for copy in put(0) + put(1):
+        copy.wait()
+
+
+def finish_kernel(gathered_hbm, totals_hbm, master_hbm, first_hbm, second_hbm,
+                  weights_hbm, master_out, first_out, second_out,
+                  gathered, weights, held, new, load_s, state_s, store_s, new_s):
+    loads, stores = [], []
+    for k in range(4):
+        layer, part = k // 2, pl.ds(k % 2 * 8, 8)
+        loads.append(pltpu.make_async_copy(gathered_hbm.at[layer, part], gathered.at[layer, part], load_s.at[k]))
+        rows = pl.ds(k % 2 * 8 * ROWS, 8 * ROWS)
+        stores.append(pltpu.make_async_copy(weights.at[layer, rows], weights_hbm.at[layer, rows], store_s.at[k]))
+    states = [
+        pltpu.make_async_copy(src, held.at[k], state_s.at[k])
+        for k, src in enumerate((totals_hbm, master_hbm, first_hbm, second_hbm))
+    ]
+    for copy in states + loads:
+        copy.start()
+    for copy in states:
+        copy.wait()
+    for k, value in enumerate(adamw(held[0], held[1], held[2], held[3])):
+        new[k] = value
+        store = pltpu.make_async_copy(new.at[k], (master_out, first_out, second_out)[k], new_s.at[k])
+        store.start()
+        stores.append(store)
+    for k in range(4):
+        loads[k].wait()
+        for two in range(k % 2 * 4, k % 2 * 4 + 4):
+            both = [gathered[k // 2, 2 * two + odd, 0:ROWS, :].astype(F32) for odd in range(2)]
+            weights[k // 2, 2 * ROWS * two : 2 * ROWS * (two + 1), :] = jnp.concatenate(both, axis=0).astype(BF16)
+        stores[k].start()
+    for copy in stores:
+        copy.wait()
 
 
 def shards(inputs, cotangent, weights, master, first_moment, second_moment):
-    whole = pl.BlockSpec(memory_space=pltpu.VMEM)
+    far = pl.BlockSpec(memory_space=pltpu.HBM)
     dma = pltpu.SemaphoreType.DMA
     vmem = pltpu.VMEM
     by_pairs = (BATCH, 16, 2, 32, CHANS)
-    new_weights, totals = pl.pallas_call(
+    gathered, totals = pl.pallas_call(
         step_kernel,
         out_shape=(
-            jax.ShapeDtypeStruct(weights.shape, BF16),
+            jax.ShapeDtypeStruct((2, 16, SLAB, CHANS), BF16),
             jax.ShapeDtypeStruct((2, ROWS, CHANS), F32),
         ),
-        in_specs=[pl.BlockSpec(memory_space=pltpu.HBM)] * 6,
-        out_specs=(whole, whole),
+        in_specs=[far] * 6,
+        out_specs=(far, far),
         scratch_shapes=[
             vmem(by_pairs, BF16),
             vmem(by_pairs, BF16),
@@ -330,18 +366,33 @@
             vmem((16, SLAB, CHANS), BF16),
             vmem((16, SLAB, CHANS), BF16),
             vmem((ROWS, CHANS), F32),
-            vmem((8, ROWS, CHANS), F32),
+            vmem((8, SLAB, CHANS), BF16),
             vmem((3, ROWS, CHANS), F32),
             vmem((2, ROWS, CHANS), F32),
             vmem((2, 16, SLAB, CHANS), BF16),
             dma((9,)),
             dma((16,)), dma((16,)), dma((16,)), dma((16,)), dma((8,)), dma((8,)), dma((4,)), dma,
-            dma((4,)), dma, dma, dma, dma((16,)), dma((16,)), dma((16,)), dma((16,)),
+            dma((4,)), dma, dma, dma, dma((16,)), dma((16,)), dma((16,)), dma((16,)), dma((2, 2)),
         ],
         compiler_params=pltpu.CompilerParams(collective_id=0, has_side_effects=True, vmem_limit_bytes=60 * 2**20),
         name="step",
     )(inputs.reshape(by_pairs), cotangent.reshape(by_pairs), weights, master, first_moment, second_moment)
-    return (new_weights,) + adamw(totals, master, first_moment, second_moment)
+    state = jax.ShapeDtypeStruct(master.shape, F32)
+    return pl.pallas_call(
+        finish_kernel,
+        out_shape=(jax.ShapeDtypeStruct(weights.shape, BF16), state, state, state),
+        in_specs=[far] * 5,
+        out_specs=(far,) * 4,
+        scratch_shapes=[
+            vmem((2, 16, SLAB, CHANS), BF16),
+            vmem(weights.shape, BF16),
+            vmem((4,) + master.shape, F32),
+            vmem((3,) + master.shape, F32),
+            dma((4,)), dma((4,)), dma((4,)), dma((3,)),
+        ],
+        compiler_params=pltpu.CompilerParams(vmem_limit_bytes=60 * 2**20),
+        name="finish",
+    )(gathered, totals, master, first_moment, second_moment)
 
 
 def solution(mesh):

time: 45.6 us -> 41.4 us (0.908)
  local copies, waits for them, and re-layouts: 1.93 us -> 0 us
  other arithmetic: 1.59 us -> 0 us
  Pallas kernels: 41.1 us -> 40.6 us
    unnamed x7 -> x0, local copies, waits for them, and re-layouts: 1.93 us -> none
    sub x1 -> x0, other arithmetic: 1.59 us -> none  [adamw(): master_new = master_part - 0.001 * (update + 0.1 * master_part)]
    pallas_call x1 -> x2, Pallas kernels: 41.1 us -> 40.6 us  [the longest x1 38.4 us: shards(): pl.pallas_call(step_kernel, out_shape=(jax.ShapeDtypeStruct((2, 16, SLAB,...]
where the time goes in v5:
time: 41.4 us; the launch traced here: 41.3 us
  Pallas kernels  40.6 us (98%)
  between operations  0.64 us (2%)
    pallas_call x1, Pallas kernels, shards(): pl.pallas_call(step_kernel, out_shape=(jax.ShapeDtypeStruct((2, 16, SLAB,...  38.4 us
    pallas_call x1, Pallas kernels, shards(): pl.pallas_call(finish_kernel, out_shape=(jax.ShapeDtypeStruct(weights.sha...  2.29 us

profile of v5, /device:TPU:1, one launch (start us, length us, event | category | flops | bytes accessed | tf_op | source)
XLA Modules:
  0.0 41.3 jit_solution(4501289359233175655)
XLA Ops:
  0.6 38.4 %step.1 = (bf16[2,16,80,128]{3,2,1,0:T(8,128)(2,1)}, f32[2,72,128]{2,1,0:T(8,128)}) custom-call(bf16[4,16,2,32,128]{4,3,2,1,0:T(8,128)(2,1)} %bitcast.2, bf16[4,16,2,32,128]{4,3,2,1,0:T(8,128)(2,1)} %bitcast.3, bf16[2,1152,128]{2,1,0:T(8,128)(2,1)} %w_hbm.1, f32[2,72,128]{2,1,0:T(8,128)} %master_hbm.3, f32[2,72,128]{2,1,0:T(8,128)} %first_hbm.3, ...), custom_call_target="tpu_custom_call" | custom-call | tf_op jit(solution)/shard_map/step/pallas_call | solution.py:344
  39.0 2.3 %finish.1 = (bf16[2,1152,128]{2,1,0:T(8,128)(2,1)}, f32[2,72,128]{2,1,0:T(8,128)}, f32[2,72,128]{2,1,0:T(8,128)}, f32[2,72,128]{2,1,0:T(8,128)}) custom-call(bf16[2,16,80,128]{3,2,1,0:T(8,128)(2,1)} %get-tuple-element.6.gathered_hbm, f32[2,72,128]{2,1,0:T(8,128)} %get-tuple-element.7.totals_hbm, f32[2,72,128]{2,1,0:T(8,128)} %master_hbm.3, ...), custom_call_target="tpu_custom_call" | custom-call | tf_op jit(solution)/shard_map/finish/pallas_call | solution.py:381

commit v6 on v5

--- a/solution.py
+++ b/solution.py
@@ -71,7 +71,7 @@
         ref[:, start : start + 512] = turned[odd * CHANS : (odd + 1) * CHANS]
 
 
-def outer_sum(turned, ref):
+def outer_sum(turned, ref, first, last):
     out = None
     for odd in range(2):
         for image in range(BATCH):
@@ -79,7 +79,9 @@
                 [ref[image, (k + odd) % 2, pl.ds((k + odd) // 2, 16)].reshape(512, 3 * CHANS) for k in range(3)], axis=1
             )
             start = odd * BATCH * 512 + image * 512
-            part = jnp.dot(turned[:, start : start + 512], near, preferred_element_type=F32)
+            part = jnp.dot(
+                turned[:, start : start + 512], near[:, first * CHANS : last * CHANS], preferred_element_type=F32
+            )
             out = part if out is None else out + part
     return out
 
@@ -134,27 +136,30 @@
     for peer in peers:
         pl.semaphore_signal(barrier, inc=1, device_id=peer, device_id_type=MESH)
 
-    def shard_rows(kx, ky):
-        start = (lax.rem(y + ky, 4) * 4 + lax.rem(x + kx, 4)) * ROWS
-        return pl.ds(pl.multiple_of(start, 8), ROWS)
-
-    def pair_copy(layer, kx, ky):
-        slot = kx * 4 + ky
-        return remote(grads.at[layer, shard_rows(kx, ky), :], pair_recv.at[slot], pair_ss.at[slot], pair_rs.at[slot], partner)
+    def place(kx, ky):
+        return lax.rem(y + ky, 4) * 4 + lax.rem(x + kx, 4)
+
+    def shard_rows(shard):
+        start = shard * ROWS
+        return pl.ds(start if isinstance(start, int) else pl.multiple_of(start, 8), ROWS)
+
+    def pair_copy(layer, shard):
+        src = grads.at[layer, shard_rows(shard), :]
+        return remote(src, pair_recv.at[shard], pair_ss.at[shard], pair_rs.at[shard], partner)
 
     def xy_copy(kx, ky):
         slot = kx * 4 + ky
         return remote(xy_send.at[slot], xy_recv.at[slot], xy_ss.at[slot], xy_rs.at[slot], xy_peer(kx, ky))
 
-    def send_pair(layer):
-        for kx, ky in xy_order + [(0, 0)]:
-            pair_copy(layer, kx, ky).start()
+    def send_pair(layer, first, last):
+        for shard in range(first, last):
+            pair_copy(layer, shard).start()
 
     def sum_pair(layer):
         for kx, ky in xy_order + [(0, 0)]:
-            slot = kx * 4 + ky
-            pair_copy(layer, kx, ky).wait_recv()
-            both = grads[layer, shard_rows(kx, ky), :] + pair_recv[slot]
+            slot, shard = kx * 4 + ky, place(kx, ky)
+            pair_copy(layer, shard).wait_recv()
+            both = grads[layer, shard_rows(shard), :] + pair_recv[shard]
             if slot:
                 xy_send[slot, 0:ROWS, :] = both.astype(BF16)
                 xy_copy(kx, ky).start()
@@ -175,6 +180,12 @@
             shift_store(x_ref, x3, image + 1)
         shift_store(c_ref, c3, image)
 
+    pair_backward(w_ref, backward_w)
+    out = outer_sum(act, c3, 0, 9)
+    for block in range(9):
+        tap = 8 - block
+        grads[1, tap * CHANS : (tap + 1) * CHANS, :] = out[:, block * CHANS : (block + 1) * CHANS]
+
     pl.semaphore_wait(barrier, len(peers))
 
     def held_copy(k, source_ref):
@@ -186,31 +197,32 @@
         for k in range(1, 4):
             held_copy(k, held).start()
 
-    pair_backward(w_ref, backward_w)
-    out = outer_sum(act, c3)
-    for block in range(9):
-        tap = 8 - block
-        grads[1, tap * CHANS : (tap + 1) * CHANS, :] = out[:, block * CHANS : (block + 1) * CHANS]
-
     @pl.when(core == 0)
     def _():
-        send_pair(1)
+        send_pair(1, 0, 16)
 
     for image in range(BATCH):
         back = jnp.dot(four_rows(c3, image), backward_w[...], preferred_element_type=F32)
         put_turned(dpre, back * slope[image], image)
 
+    def first_layer(first, last):
+        out = outer_sum(dpre, x3, first, last)
+        for tap in range(first, last):
+            block = out[:, (tap - first) * CHANS : (tap + 1 - first) * CHANS]
+            grads[0, tap * CHANS : (tap + 1) * CHANS, :] = block.T
+
+    first_layer(0, 4)
+
     @pl.when(core == 1)
     def _():
+        send_pair(0, 0, 7)
+
+    first_layer(4, 9)
+
+    @pl.when(core == 1)
+    def _():
+        send_pair(0, 7, 16)
         sum_pair(1)
-
-    out = outer_sum(dpre, x3)
-    for tap in range(9):
-        grads[0, tap * CHANS : (tap + 1) * CHANS, :] = out[:, tap * CHANS : (tap + 1) * CHANS].T
-
-    @pl.when(core == 1)
-    def _():
-        send_pair(0)
 
     @pl.when(core == 0)
     def _():
@@ -232,64 +244,68 @@
     z_part = [z_parts[k, 0:ROWS, :].astype(F32) for k in range(8)]
     halves = [(z_part[k] + z_part[k + 1]) + (z_part[k + 2] + z_part[k + 3]) for k in (0, 4)]
     whole = halves[0] + halves[1]
+
     @pl.when(z_lo != y)
     def _():
         held_copy(1, held).wait_recv()
 
     slab = adamw(whole, held[0], held[1], held[2])[0].astype(BF16)
-    gathered[core, y * 4 + x, 0:ROWS, :] = slab
+    gathered[y * 4 + x, 0:ROWS, :] = slab
 
     def gat_copy(kx, ky, slot):
-        return remote(slot, slot, gat_ss.at[kx * 4 + ky], gat_rs.at[kx * 4 + ky], xy_peer(kx, ky))
-
-    def source(layer, kx, ky):
-        return gathered.at[layer, lax.rem(y + 4 - ky, 4) * 4 + lax.rem(x + 4 - kx, 4)]
+        ref = gathered.at[slot]
+        return remote(ref, ref, gat_ss.at[kx * 4 + ky], gat_rs.at[kx * 4 + ky], xy_peer(kx, ky))
+
+    def source(kx, ky):
+        return place(4 - kx, 4 - ky)
 
     def fwd_copy(layer, kx, ky):
-        slot = source(layer, kx, ky)
-        return remote(slot, slot, fwd_ss.at[kx * 4 + ky], fwd_rs.at[kx * 4 + ky], partner)
+        slot = source(kx, ky)
+        k = kx * 4 + ky
+        return remote(gathered.at[slot], gathered_out.at[layer, slot], fwd_ss.at[k], fwd_rs.at[k], partner)
 
     for kx, ky in xy_order:
-        gat_copy(kx, ky, source(core, 0, 0)).start()
+        gat_copy(kx, ky, source(0, 0)).start()
     fwd_copy(core, 0, 0).start()
 
     def t_copy(ky):
-        return remote(totals.at[core], totals.at[core], t_ss.at[ky], t_rs, xy_peer(0, ky))
+        return remote(totals, totals, t_ss.at[ky], t_rs, xy_peer(0, ky))
 
     @pl.when(z_lo == y)
     def _():
-        totals[core] = whole
+        totals[...] = whole
         for ky in (2, 1, 3):
             t_copy(ky).start()
 
+    def forward(steps):
+        for kx, ky in steps:
+            gat_copy(kx, ky, source(kx, ky)).wait_recv()
+            fwd_copy(core, kx, ky).start()
+
+    forward(xy_steps[:3])
+
     @pl.when(z_lo != y)
     def _():
         t_copy(1).wait_recv()
 
-    tot = remote(totals.at[core], totals.at[core], tot_ss, tot_rs, partner)
+    tot = remote(totals, totals_out.at[core], tot_ss, tot_rs, partner)
     tot.start()
-
-    def put(layer):
-        pairs = ((gathered.at[layer], gathered_out.at[layer]), (totals.at[layer], totals_out.at[layer]))
-        return [pltpu.make_async_copy(src, dst, put_s.at[layer, k]) for k, (src, dst) in enumerate(pairs)]
-
-    for kx, ky in xy_steps:
-        gat_copy(kx, ky, source(core, kx, ky)).wait_recv()
-        fwd_copy(core, kx, ky).start()
-    for copy in put(core):
-        copy.start()
-    remote(totals.at[1 - core], totals.at[1 - core], tot_ss, tot_rs, partner).wait_recv()
+    puts = [
+        pltpu.make_async_copy(totals, totals_out.at[core], put_s.at[0]),
+        pltpu.make_async_copy(gathered, gathered_out.at[core], put_s.at[1]),
+    ]
+    puts[0].start()
+    forward(xy_steps[3:])
+    puts[1].start()
+    remote(totals, totals_out.at[1 - core], tot_ss, tot_rs, partner).wait_recv()
     for kx, ky in xy_steps + [(0, 0)]:
         fwd_copy(1 - core, kx, ky).wait_recv()
-    for copy in put(1 - core):
-        copy.start()
-    for kx in range(4):
-        for k in range(4):
-            pair_copy(1 - core, kx, k).wait_send()
-            fwd_copy(core, kx, k).wait_send()
+    for k in range(16):
+        pair_copy(1 - core, k).wait_send()
+        fwd_copy(core, k // 4, k % 4).wait_send()
     for kx, ky in xy_steps:
         xy_copy(kx, ky).wait_send()
-        gat_copy(kx, ky, source(core, 0, 0)).wait_send()
+        gat_copy(kx, ky, source(0, 0)).wait_send()
     for kz in z_order:
         z_copy(kz, z).wait_send()
 
@@ -300,7 +316,7 @@
             t_copy(k).wait_send()
 
     tot.wait_send()
-    for copy in put(0) + put(1):
+    for copy in puts:
         copy.wait()
 
 
@@ -368,11 +384,11 @@
             vmem((ROWS, CHANS), F32),
             vmem((8, SLAB, CHANS), BF16),
             vmem((3, ROWS, CHANS), F32),
-            vmem((2, ROWS, CHANS), F32),
-            vmem((2, 16, SLAB, CHANS), BF16),
+            vmem((ROWS, CHANS), F32),
+            vmem((16, SLAB, CHANS), BF16),
             dma((9,)),
             dma((16,)), dma((16,)), dma((16,)), dma((16,)), dma((8,)), dma((8,)), dma((4,)), dma,
-            dma((4,)), dma, dma, dma, dma((16,)), dma((16,)), dma((16,)), dma((16,)), dma((2, 2)),
+            dma((4,)), dma, dma, dma, dma((16,)), dma((16,)), dma((16,)), dma((16,)), dma((2,)),
         ],
         compiler_params=pltpu.CompilerParams(collective_id=0, has_side_effects=True, vmem_limit_bytes=60 * 2**20),
         name="step",

time: 41.4 us -> 40.5 us (0.978)
  Pallas kernels: 40.6 us -> 39.8 us
    pallas_call x1, Pallas kernels: 38.4 us -> 37.5 us  [shards(): pl.pallas_call(step_kernel, out_shape=(jax.ShapeDtypeStruct((2, 16, SLAB,...]
where the time goes in v6:
time: 40.5 us; the launch traced here: 40.4 us
  Pallas kernels  39.8 us (98%)
  between operations  0.64 us (2%)
    pallas_call x1, Pallas kernels, shards(): pl.pallas_call(step_kernel, out_shape=(jax.ShapeDtypeStruct((2, 16, SLAB,...  37.5 us
    pallas_call x1, Pallas kernels, shards(): pl.pallas_call(finish_kernel, out_shape=(jax.ShapeDtypeStruct(weights.sha...  2.29 us

profile of v6, /device:TPU:1, one launch (start us, length us, event | category | flops | bytes accessed | tf_op | source)
XLA Modules:
  0.0 40.4 jit_solution(2742660652725596071)
XLA Ops:
  0.6 37.5 %step.1 = (bf16[2,16,80,128]{3,2,1,0:T(8,128)(2,1)}, f32[2,72,128]{2,1,0:T(8,128)}) custom-call(bf16[4,16,2,32,128]{4,3,2,1,0:T(8,128)(2,1)} %bitcast.2, bf16[4,16,2,32,128]{4,3,2,1,0:T(8,128)(2,1)} %bitcast.3, bf16[2,1152,128]{2,1,0:T(8,128)(2,1)} %w_hbm.1, f32[2,72,128]{2,1,0:T(8,128)} %master_hbm.3, f32[2,72,128]{2,1,0:T(8,128)} %first_hbm.3, ...), custom_call_target="tpu_custom_call" | custom-call | tf_op jit(solution)/shard_map/step/pallas_call | solution.py:360
  38.1 2.3 %finish.1 = (bf16[2,1152,128]{2,1,0:T(8,128)(2,1)}, f32[2,72,128]{2,1,0:T(8,128)}, f32[2,72,128]{2,1,0:T(8,128)}, f32[2,72,128]{2,1,0:T(8,128)}) custom-call(bf16[2,16,80,128]{3,2,1,0:T(8,128)(2,1)} %get-tuple-element.6.gathered_hbm, f32[2,72,128]{2,1,0:T(8,128)} %get-tuple-element.7.totals_hbm, f32[2,72,128]{2,1,0:T(8,128)} %master_hbm.3, ...), custom_call_target="tpu_custom_call" | custom-call | tf_op jit(solution)/shard_map/finish/pallas_call | solution.py:397

commit v7 on v6

--- a/solution.py
+++ b/solution.py
@@ -90,8 +90,8 @@
                 gathered_out, totals_out,
                 x_ref, c_ref, w_ref, state_ref,
                 x3, c3, forward_w, backward_w, act, slope, dpre, grads,
-                pair_recv, xy_send, xy_recv, xy_own, z_parts, held, totals, gathered,
-                load_s, pair_ss, pair_rs, xy_ss, xy_rs, z_ss, z_rs, held_ss, held_rs, t_ss, t_rs, tot_ss, tot_rs,
+                xy_send, xy_recv, z_parts, held, totals, gathered,
+                load_s, xy_ss, xy_rs, z_ss, z_rs, held_ss, held_rs, t_ss, t_rs, tot_ss, tot_rs,
                 gat_ss, gat_rs, fwd_ss, fwd_rs, put_s):
     grp = lax.axis_index("grp")
     dev = lax.axis_index("dev")
@@ -103,8 +103,8 @@
     z = z_hi * 4 + z_lo
     partner = (grp + 1 - 2 * core, dev)
 
-    def xy_peer(kx, ky):
-        return (z_hi * 8 + lax.rem(y + ky, 4) * 2 + core, z_lo * 4 + lax.rem(x + kx, 4))
+    def xy_peer(kx, ky, at=core):
+        return (z_hi * 8 + lax.rem(y + ky, 4) * 2 + at, z_lo * 4 + lax.rem(x + kx, 4))
 
     def z_peer(kz):
         other = lax.rem(z + kz, 8)
@@ -131,7 +131,7 @@
     xy_order = [(kx, ky) for kx in (2, 1, 3, 0) for ky in (2, 1, 3, 0) if kx or ky]
     xy_steps = [(kx, ky) for kx in (0, 1, 3, 2) for ky in (0, 1, 3, 2) if kx or ky]
     z_order = (4, 3, 5, 2, 6, 1, 7)
-    peers = [partner] + [xy_peer(*k) for k in xy_steps] + [z_peer(k) for k in z_order]
+    peers = [partner] + [xy_peer(*k, at) for k in xy_steps for at in range(2)] + [z_peer(k) for k in z_order]
     barrier = pltpu.get_barrier_semaphore()
     for peer in peers:
         pl.semaphore_signal(barrier, inc=1, device_id=peer, device_id_type=MESH)
@@ -143,28 +143,24 @@
         start = shard * ROWS
         return pl.ds(start if isinstance(start, int) else pl.multiple_of(start, 8), ROWS)
 
-    def pair_copy(layer, shard):
-        src = grads.at[layer, shard_rows(shard), :]
-        return remote(src, pair_recv.at[shard], pair_ss.at[shard], pair_rs.at[shard], partner)
-
-    def xy_copy(kx, ky):
-        slot = kx * 4 + ky
-        return remote(xy_send.at[slot], xy_recv.at[slot], xy_ss.at[slot], xy_rs.at[slot], xy_peer(kx, ky))
-
-    def send_pair(layer, first, last):
+    own = y * 4 + x
+
+    def xy_copy(layer, shard):
+        other = 1 - core if layer else core
+        kx, ky = lax.rem(shard % 4 + 4 - x, 4), lax.rem(shard // 4 + 4 - y, 4)
+        slot = other * 16 + kx * 4 + ky
+        target = (z_hi * 8 + shard // 4 * 2 + layer, z_lo * 4 + shard % 4)
+        copy = remote(xy_send.at[layer, shard], xy_recv.at[slot], xy_ss.at[layer, shard], xy_rs.at[slot], target)
+        return copy, slot > 0
+
+    def send_parts(layer, first, last):
         for shard in range(first, last):
-            pair_copy(layer, shard).start()
-
-    def sum_pair(layer):
-        for kx, ky in xy_order + [(0, 0)]:
-            slot, shard = kx * 4 + ky, place(kx, ky)
-            pair_copy(layer, shard).wait_recv()
-            both = grads[layer, shard_rows(shard), :] + pair_recv[shard]
-            if slot:
-                xy_send[slot, 0:ROWS, :] = both.astype(BF16)
-                xy_copy(kx, ky).start()
-            else:
-                xy_own[...] = both
+            copy, remote_one = xy_copy(layer, shard)
+            pl.when(remote_one)(copy.start)
+
+    def round_parts(layer, first, last):
+        for shard in range(first, last):
+            xy_send[layer, shard, 0:ROWS, :] = grads[layer, shard_rows(shard), :].astype(BF16)
 
     for copy in loads:
         copy.wait()
@@ -185,8 +181,10 @@
     for block in range(9):
         tap = 8 - block
         grads[1, tap * CHANS : (tap + 1) * CHANS, :] = out[:, block * CHANS : (block + 1) * CHANS]
+    round_parts(1, 0, 16)
 
     pl.semaphore_wait(barrier, len(peers))
+    send_parts(1, 0, 16)
 
     def held_copy(k, source_ref):
         return remote(source_ref, held, held_ss.at[k], held_rs, held_peer(k))
@@ -197,10 +195,6 @@
         for k in range(1, 4):
             held_copy(k, held).start()
 
-    @pl.when(core == 0)
-    def _():
-        send_pair(1, 0, 16)
-
     for image in range(BATCH):
         back = jnp.dot(four_rows(c3, image), backward_w[...], preferred_element_type=F32)
         put_turned(dpre, back * slope[image], image)
@@ -212,26 +206,20 @@
             grads[0, tap * CHANS : (tap + 1) * CHANS, :] = block.T
 
     first_layer(0, 4)
-
-    @pl.when(core == 1)
-    def _():
-        send_pair(0, 0, 7)
-
+    round_parts(0, 0, 7)
+    send_parts(0, 0, 7)
     first_layer(4, 9)
-
-    @pl.when(core == 1)
-    def _():
-        send_pair(0, 7, 16)
-        sum_pair(1)
-
-    @pl.when(core == 0)
-    def _():
-        sum_pair(0)
-
-    acc = xy_own[...]
-    for kx, ky in xy_steps:
-        xy_copy(kx, ky).wait_recv()
-        acc = acc + xy_recv[kx * 4 + ky, 0:ROWS, :].astype(F32)
+    round_parts(0, 7, 16)
+    send_parts(0, 7, 16)
+
+    acc = grads[core, shard_rows(own), :]
+    for kx, ky in [(0, 0)] + xy_steps:
+        for other in range(2):
+            slot = other * 16 + kx * 4 + ky
+            if slot:
+                ref = xy_recv.at[slot]
+                remote(ref, ref, xy_ss.at[0, 0], xy_rs.at[slot], partner).wait_recv()
+                acc = acc + xy_recv[slot, 0:ROWS, :].astype(F32)
     z_parts[z, 0:ROWS, :] = acc.astype(BF16)
 
     def z_copy(kz, place):
@@ -301,10 +289,11 @@
     for kx, ky in xy_steps + [(0, 0)]:
         fwd_copy(1 - core, kx, ky).wait_recv()
     for k in range(16):
-        pair_copy(1 - core, k).wait_send()
         fwd_copy(core, k // 4, k % 4).wait_send()
+        for layer in range(2):
+            copy, remote_one = xy_copy(layer, k)
+            pl.when(remote_one)(copy.wait_send)
     for kx, ky in xy_steps:
-        xy_copy(kx, ky).wait_send()
         gat_copy(kx, ky, source(0, 0)).wait_send()
     for kz in z_order:
         z_copy(kz, z).wait_send()
@@ -378,16 +367,14 @@
             vmem((BATCH, 512, 2 * CHANS), F32),
             vmem((CHANS, BATCH * 1024), BF16),
             vmem((2, 9 * CHANS, CHANS), F32),
-            vmem((16, ROWS, CHANS), F32),
-            vmem((16, SLAB, CHANS), BF16),
-            vmem((16, SLAB, CHANS), BF16),
-            vmem((ROWS, CHANS), F32),
+            vmem((2, 16, SLAB, CHANS), BF16),
+            vmem((32, SLAB, CHANS), BF16),
             vmem((8, SLAB, CHANS), BF16),
             vmem((3, ROWS, CHANS), F32),
             vmem((ROWS, CHANS), F32),
             vmem((16, SLAB, CHANS), BF16),
             dma((9,)),
-            dma((16,)), dma((16,)), dma((16,)), dma((16,)), dma((8,)), dma((8,)), dma((4,)), dma,
+            dma((2, 16)), dma((32,)), dma((8,)), dma((8,)), dma((4,)), dma,
             dma((4,)), dma, dma, dma, dma((16,)), dma((16,)), dma((16,)), dma((16,)), dma((2,)),
         ],
         compiler_params=pltpu.CompilerParams(collective_id=0, has_side_effects=True, vmem_limit_bytes=60 * 2**20),

time: 40.5 us -> 40.7 us (level)
  no operation moved by 1% of the time
where the time goes in v7:
time: 40.7 us; the launch traced here: 40.5 us
  Pallas kernels  39.9 us (98%)
  between operations  0.64 us (2%)
    pallas_call x1, Pallas kernels, shards(): pl.pallas_call(step_kernel, out_shape=(jax.ShapeDtypeStruct((2, 16, SLAB,...  37.6 us
    pallas_call x1, Pallas kernels, shards(): pl.pallas_call(finish_kernel, out_shape=(jax.ShapeDtypeStruct(weights.sha...  2.29 us

profile of v7, /device:TPU:1, one launch (start us, length us, event | category | flops | bytes accessed | tf_op | source)
XLA Modules:
  0.0 40.5 jit_solution(17878932454024468014)
XLA Ops:
  0.6 37.6 %step.1 = (bf16[2,16,80,128]{3,2,1,0:T(8,128)(2,1)}, f32[2,72,128]{2,1,0:T(8,128)}) custom-call(bf16[4,16,2,32,128]{4,3,2,1,0:T(8,128)(2,1)} %bitcast.2, bf16[4,16,2,32,128]{4,3,2,1,0:T(8,128)(2,1)} %bitcast.3, bf16[2,1152,128]{2,1,0:T(8,128)(2,1)} %w_hbm.1, f32[2,72,128]{2,1,0:T(8,128)} %master_hbm.3, f32[2,72,128]{2,1,0:T(8,128)} %first_hbm.3, ...), custom_call_target="tpu_custom_call" | custom-call | tf_op jit(solution)/shard_map/step/pallas_call | solution.py:349
  38.3 2.3 %finish.1 = (bf16[2,1152,128]{2,1,0:T(8,128)(2,1)}, f32[2,72,128]{2,1,0:T(8,128)}, f32[2,72,128]{2,1,0:T(8,128)}, f32[2,72,128]{2,1,0:T(8,128)}) custom-call(bf16[2,16,80,128]{3,2,1,0:T(8,128)(2,1)} %get-tuple-element.6.gathered_hbm, f32[2,72,128]{2,1,0:T(8,128)} %get-tuple-element.7.totals_hbm, f32[2,72,128]{2,1,0:T(8,128)} %master_hbm.3, ...), custom_call_target="tpu_custom_call" | custom-call | tf_op jit(solution)/shard_map/finish/pallas_call | solution.py:384

commit v8 on v7

--- a/solution.py
+++ b/solution.py
@@ -121,12 +121,12 @@
     loads = [
         pltpu.make_async_copy(src, dst, load_s.at[k])
         for k, (src, dst) in enumerate(
-            [(x_hbm, x_ref), (w_hbm, w_ref), (c_hbm, c_ref)]
+            [(w_hbm.at[0], w_ref.at[0]), (x_hbm, x_ref), (c_hbm, c_ref), (w_hbm.at[1], w_ref.at[1])]
             + [(ref.at[layer], state_ref.at[layer, k])
                for k, ref in enumerate((master_hbm, first_hbm, second_hbm)) for layer in range(2)]
         )
     ]
-    for copy in loads:
+    for copy in loads[:2]:
         copy.start()
     xy_order = [(kx, ky) for kx in (2, 1, 3, 0) for ky in (2, 1, 3, 0) if kx or ky]
     xy_steps = [(kx, ky) for kx in (0, 1, 3, 2) for ky in (0, 1, 3, 2) if kx or ky]
@@ -162,8 +162,10 @@
         for shard in range(first, last):
             xy_send[layer, shard, 0:ROWS, :] = grads[layer, shard_rows(shard), :].astype(BF16)
 
-    for copy in loads:
+    for copy in loads[:2]:
         copy.wait()
+    for copy in loads[2:]:
+        copy.start()
     pair_forward(w_ref, forward_w)
     shift_store(x_ref, x3, 0)
     for image in range(BATCH):
@@ -174,17 +176,25 @@
         slope[image] = sig + value * (1.0 - sig)
         if image < BATCH - 1:
             shift_store(x_ref, x3, image + 1)
+    for copy in loads[2:]:
+        copy.wait()
+    pl.semaphore_wait(barrier, len(peers))
+    pair_backward(w_ref, backward_w)
+    for image in range(BATCH):
         shift_store(c_ref, c3, image)
 
-    pair_backward(w_ref, backward_w)
-    out = outer_sum(act, c3, 0, 9)
-    for block in range(9):
-        tap = 8 - block
-        grads[1, tap * CHANS : (tap + 1) * CHANS, :] = out[:, block * CHANS : (block + 1) * CHANS]
-    round_parts(1, 0, 16)
-
-    pl.semaphore_wait(barrier, len(peers))
-    send_parts(1, 0, 16)
+    def second_layer(first, last):
+        out = outer_sum(act, c3, first, last)
+        for block in range(first, last):
+            tap = 8 - block
+            grads[1, tap * CHANS : (tap + 1) * CHANS, :] = out[:, (block - first) * CHANS : (block - first + 1) * CHANS]
+
+    second_layer(0, 5)
+    round_parts(1, 8, 16)
+    send_parts(1, 8, 16)
+    second_layer(5, 9)
+    round_parts(1, 0, 8)
+    send_parts(1, 0, 8)
 
     def held_copy(k, source_ref):
         return remote(source_ref, held, held_ss.at[k], held_rs, held_peer(k))
@@ -205,12 +215,12 @@
             block = out[:, (tap - first) * CHANS : (tap + 1 - first) * CHANS]
             grads[0, tap * CHANS : (tap + 1) * CHANS, :] = block.T
 
-    first_layer(0, 4)
-    round_parts(0, 0, 7)
-    send_parts(0, 0, 7)
-    first_layer(4, 9)
-    round_parts(0, 7, 16)
-    send_parts(0, 7, 16)
+    first_layer(0, 5)
+    round_parts(0, 0, 8)
+    send_parts(0, 0, 8)
+    first_layer(5, 9)
+    round_parts(0, 8, 16)
+    send_parts(0, 8, 16)
 
     acc = grads[core, shard_rows(own), :]
     for kx, ky in [(0, 0)] + xy_steps:
@@ -222,27 +232,39 @@
                 acc = acc + xy_recv[slot, 0:ROWS, :].astype(F32)
     z_parts[z, 0:ROWS, :] = acc.astype(BF16)
 
-    def z_copy(kz, place):
-        return remote(z_parts.at[place], z_parts.at[place], z_ss.at[kz], z_rs.at[kz], z_peer(kz))
-
-    for kz in z_order:
-        z_copy(kz, z).start()
-    for kz in z_order[::-1]:
-        z_copy(kz, lax.rem(z + 8 - kz, 8)).wait_recv()
-    z_part = [z_parts[k, 0:ROWS, :].astype(F32) for k in range(8)]
-    halves = [(z_part[k] + z_part[k + 1]) + (z_part[k + 2] + z_part[k + 3]) for k in (0, 4)]
-    whole = halves[0] + halves[1]
+    parts = (pl.ds(0, 32), pl.ds(32, SLAB - 32))
+
+    def z_copy(kz, place, part):
+        ref = z_parts.at[place, parts[part]]
+        return remote(ref, ref, z_ss.at[part, kz], z_rs.at[part, kz], z_peer(kz))
+
+    def gat_copy(kx, ky, slot, part):
+        ref = gathered.at[slot, parts[part]]
+        k = kx * 4 + ky
+        return remote(ref, ref, gat_ss.at[part, k], gat_rs.at[part, k], xy_peer(kx, ky))
+
+    for part in range(2):
+        for kz in z_order:
+            z_copy(kz, z, part).start()
 
     @pl.when(z_lo != y)
     def _():
         held_copy(1, held).wait_recv()
 
-    slab = adamw(whole, held[0], held[1], held[2])[0].astype(BF16)
-    gathered[y * 4 + x, 0:ROWS, :] = slab
-
-    def gat_copy(kx, ky, slot):
-        ref = gathered.at[slot]
-        return remote(ref, ref, gat_ss.at[kx * 4 + ky], gat_rs.at[kx * 4 + ky], xy_peer(kx, ky))
+    for part, rows in enumerate((pl.ds(0, 32), pl.ds(32, ROWS - 32))):
+        for kz in z_order[::-1]:
+            z_copy(kz, lax.rem(z + 8 - kz, 8), part).wait_recv()
+        z_part = [z_parts[k, rows, :].astype(F32) for k in range(8)]
+        halves = [(z_part[k] + z_part[k + 1]) + (z_part[k + 2] + z_part[k + 3]) for k in (0, 4)]
+        whole = halves[0] + halves[1]
+
+        @pl.when(z_lo == y)
+        def _(rows=rows, whole=whole):
+            totals[rows, :] = whole
+
+        gathered[own, rows, :] = adamw(whole, held[0, rows, :], held[1, rows, :], held[2, rows, :])[0].astype(BF16)
+        for kx, ky in xy_order:
+            gat_copy(kx, ky, own, part).start()
 
     def source(kx, ky):
         return place(4 - kx, 4 - ky)
@@ -252,8 +274,6 @@
         k = kx * 4 + ky
         return remote(gathered.at[slot], gathered_out.at[layer, slot], fwd_ss.at[k], fwd_rs.at[k], partner)
 
-    for kx, ky in xy_order:
-        gat_copy(kx, ky, source(0, 0)).start()
     fwd_copy(core, 0, 0).start()
 
     def t_copy(ky):
@@ -261,13 +281,13 @@
 
     @pl.when(z_lo == y)
     def _():
-        totals[...] = whole
         for ky in (2, 1, 3):
             t_copy(ky).start()
 
     def forward(steps):
         for kx, ky in steps:
-            gat_copy(kx, ky, source(kx, ky)).wait_recv()
+            for part in range(2):
+                gat_copy(kx, ky, source(kx, ky), part).wait_recv()
             fwd_copy(core, kx, ky).start()
 
     forward(xy_steps[:3])
@@ -294,9 +314,11 @@
             copy, remote_one = xy_copy(layer, k)
             pl.when(remote_one)(copy.wait_send)
     for kx, ky in xy_steps:
-        gat_copy(kx, ky, source(0, 0)).wait_send()
+        for part in range(2):
+            gat_copy(kx, ky, own, part).wait_send()
     for kz in z_order:
-        z_copy(kz, z).wait_send()
+        for part in range(2):
+            z_copy(kz, z, part).wait_send()
 
     @pl.when(z_lo == y)
     def _():
@@ -373,9 +395,9 @@
             vmem((3, ROWS, CHANS), F32),
             vmem((ROWS, CHANS), F32),
             vmem((16, SLAB, CHANS), BF16),
-            dma((9,)),
-            dma((2, 16)), dma((32,)), dma((8,)), dma((8,)), dma((4,)), dma,
-            dma((4,)), dma, dma, dma, dma((16,)), dma((16,)), dma((16,)), dma((16,)), dma((2,)),
+            dma((10,)),
+            dma((2, 16)), dma((32,)), dma((2, 8)), dma((2, 8)), dma((4,)), dma,
+            dma((4,)), dma, dma, dma, dma((2, 16)), dma((2, 16)), dma((16,)), dma((16,)), dma((2,)),
         ],
         compiler_params=pltpu.CompilerParams(collective_id=0, has_side_effects=True, vmem_limit_bytes=60 * 2**20),
         name="step",

time: 40.7 us -> 41.1 us (level)
  no operation moved by 1% of the time
where the time goes in v8:
time: 41.1 us; the launch traced here: 40.9 us
  Pallas kernels  40.3 us (98%)
  between operations  0.64 us (2%)
    pallas_call x1, Pallas kernels, shards(): pl.pallas_call(step_kernel, out_shape=(jax.ShapeDtypeStruct((2, 16, SLAB,...  38 us
    pallas_call x1, Pallas kernels, shards(): pl.pallas_call(finish_kernel, out_shape=(jax.ShapeDtypeStruct(weights.sha...  2.29 us

profile of v8, /device:TPU:1, one launch (start us, length us, event | category | flops | bytes accessed | tf_op | source)
XLA Modules:
  0.0 40.9 jit_solution(7856621785871156665)
XLA Ops:
  0.6 38.0 %step.1 = (bf16[2,16,80,128]{3,2,1,0:T(8,128)(2,1)}, f32[2,72,128]{2,1,0:T(8,128)}) custom-call(bf16[4,16,2,32,128]{4,3,2,1,0:T(8,128)(2,1)} %bitcast.2, bf16[4,16,2,32,128]{4,3,2,1,0:T(8,128)(2,1)} %bitcast.3, bf16[2,1152,128]{2,1,0:T(8,128)(2,1)} %w_hbm.1, f32[2,72,128]{2,1,0:T(8,128)} %master_hbm.3, f32[2,72,128]{2,1,0:T(8,128)} %first_hbm.3, ...), custom_call_target="tpu_custom_call" | custom-call | tf_op jit(solution)/shard_map/step/pallas_call | solution.py:371
  38.6 2.3 %finish.1 = (bf16[2,1152,128]{2,1,0:T(8,128)(2,1)}, f32[2,72,128]{2,1,0:T(8,128)}, f32[2,72,128]{2,1,0:T(8,128)}, f32[2,72,128]{2,1,0:T(8,128)}) custom-call(bf16[2,16,80,128]{3,2,1,0:T(8,128)(2,1)} %get-tuple-element.6.gathered_hbm, f32[2,72,128]{2,1,0:T(8,128)} %get-tuple-element.7.totals_hbm, f32[2,72,128]{2,1,0:T(8,128)} %master_hbm.3, ...), custom_call_target="tpu_custom_call" | custom-call | tf_op jit(solution)/shard_map/finish/pallas_call | solution.py:406

commit v9 on v7

--- a/solution.py
+++ b/solution.py
@@ -90,8 +90,8 @@
                 gathered_out, totals_out,
                 x_ref, c_ref, w_ref, state_ref,
                 x3, c3, forward_w, backward_w, act, slope, dpre, grads,
-                xy_send, xy_recv, z_parts, held, totals, gathered,
-                load_s, xy_ss, xy_rs, z_ss, z_rs, held_ss, held_rs, t_ss, t_rs, tot_ss, tot_rs,
+                pair_recv, xy_send, xy_recv, z_parts, held, totals, gathered,
+                load_s, pair_ss, pair_rs, xy_ss, xy_rs, z_ss, z_rs, held_ss, held_rs, t_ss, t_rs, tot_ss, tot_rs,
                 gat_ss, gat_rs, fwd_ss, fwd_rs, put_s):
     grp = lax.axis_index("grp")
     dev = lax.axis_index("dev")
@@ -146,12 +146,35 @@
     own = y * 4 + x
 
     def xy_copy(layer, shard):
-        other = 1 - core if layer else core
+        other = 1 - core
         kx, ky = lax.rem(shard % 4 + 4 - x, 4), lax.rem(shard // 4 + 4 - y, 4)
         slot = other * 16 + kx * 4 + ky
         target = (z_hi * 8 + shard // 4 * 2 + layer, z_lo * 4 + shard % 4)
         copy = remote(xy_send.at[layer, shard], xy_recv.at[slot], xy_ss.at[layer, shard], xy_rs.at[slot], target)
         return copy, slot > 0
+
+    def pair_copy(shard):
+        return remote(grads.at[0, shard_rows(shard), :], pair_recv.at[shard], pair_ss.at[shard], pair_rs.at[shard], partner)
+
+    def send_pair(first, last):
+        for shard in range(first, last):
+            pair_copy(shard).start()
+
+    def pair_xy_copy(kx, ky):
+        slot, shard = kx * 4 + ky, place(kx, ky)
+        target = xy_peer(kx, ky)
+        return remote(xy_send.at[0, shard], xy_recv.at[slot], xy_ss.at[0, shard], xy_rs.at[slot], target)
+
+    def sum_pair():
+        for kx, ky in xy_order + [(0, 0)]:
+            shard = place(kx, ky)
+            pair_copy(shard).wait_recv()
+            both = grads[0, shard_rows(shard), :] + pair_recv[shard]
+            if kx or ky:
+                xy_send[0, shard, 0:ROWS, :] = both.astype(BF16)
+                pair_xy_copy(kx, ky).start()
+            else:
+                grads[0, shard_rows(shard), :] = both
 
     def send_parts(layer, first, last):
         for shard in range(first, last):
@@ -205,22 +228,40 @@
             block = out[:, (tap - first) * CHANS : (tap + 1 - first) * CHANS]
             grads[0, tap * CHANS : (tap + 1) * CHANS, :] = block.T
 
-    first_layer(0, 4)
-    round_parts(0, 0, 7)
-    send_parts(0, 0, 7)
-    first_layer(4, 9)
-    round_parts(0, 7, 16)
-    send_parts(0, 7, 16)
-
-    acc = grads[core, shard_rows(own), :]
-    for kx, ky in [(0, 0)] + xy_steps:
-        for other in range(2):
-            slot = other * 16 + kx * 4 + ky
-            if slot:
-                ref = xy_recv.at[slot]
-                remote(ref, ref, xy_ss.at[0, 0], xy_rs.at[slot], partner).wait_recv()
-                acc = acc + xy_recv[slot, 0:ROWS, :].astype(F32)
-    z_parts[z, 0:ROWS, :] = acc.astype(BF16)
+    first_layer(0, 5)
+
+    @pl.when(core == 1)
+    def _():
+        send_pair(0, 8)
+
+    first_layer(5, 9)
+
+    @pl.when(core == 1)
+    def _():
+        send_pair(8, 16)
+
+    @pl.when(core == 0)
+    def _():
+        sum_pair()
+
+    def sum_parts(layer, others):
+        acc = grads[layer, shard_rows(own), :]
+        for kx, ky in [(0, 0)] + xy_steps:
+            for other in range(others):
+                slot = other * 16 + kx * 4 + ky
+                if slot:
+                    ref = xy_recv.at[slot]
+                    remote(ref, ref, xy_ss.at[0, 0], xy_rs.at[slot], partner).wait_recv()
+                    acc = acc + xy_recv[slot, 0:ROWS, :].astype(F32)
+        z_parts[z, 0:ROWS, :] = acc.astype(BF16)
+
+    @pl.when(core == 0)
+    def _():
+        sum_parts(0, 1)
+
+    @pl.when(core == 1)
+    def _():
+        sum_parts(1, 2)
 
     def z_copy(kz, place):
         return remote(z_parts.at[place], z_parts.at[place], z_ss.at[kz], z_rs.at[kz], z_peer(kz))
@@ -290,11 +331,21 @@
         fwd_copy(1 - core, kx, ky).wait_recv()
     for k in range(16):
         fwd_copy(core, k // 4, k % 4).wait_send()
-        for layer in range(2):
-            copy, remote_one = xy_copy(layer, k)
-            pl.when(remote_one)(copy.wait_send)
+        copy, remote_one = xy_copy(1, k)
+        pl.when(remote_one)(copy.wait_send)
     for kx, ky in xy_steps:
         gat_copy(kx, ky, source(0, 0)).wait_send()
+
+    @pl.when(core == 0)
+    def _():
+        for kx, ky in xy_steps:
+            pair_xy_copy(kx, ky).wait_send()
+
+    @pl.when(core == 1)
+    def _():
+        for k in range(16):
+            pair_copy(k).wait_send()
+
     for kz in z_order:
         z_copy(kz, z).wait_send()
 
@@ -367,6 +418,7 @@
             vmem((BATCH, 512, 2 * CHANS), F32),
             vmem((CHANS, BATCH * 1024), BF16),
             vmem((2, 9 * CHANS, CHANS), F32),
+            vmem((16, ROWS, CHANS), F32),
             vmem((2, 16, SLAB, CHANS), BF16),
             vmem((32, SLAB, CHANS), BF16),
             vmem((8, SLAB, CHANS), BF16),
@@ -374,7 +426,7 @@
             vmem((ROWS, CHANS), F32),
             vmem((16, SLAB, CHANS), BF16),
             dma((9,)),
-            dma((2, 16)), dma((32,)), dma((8,)), dma((8,)), dma((4,)), dma,
+            dma((16,)), dma((16,)), dma((2, 16)), dma((32,)), dma((8,)), dma((8,)), dma((4,)), dma,
             dma((4,)), dma, dma, dma, dma((16,)), dma((16,)), dma((16,)), dma((16,)), dma((2,)),
         ],
         compiler_params=pltpu.CompilerParams(collective_id=0, has_side_effects=True, vmem_limit_bytes=60 * 2**20),

time: 40.7 us -> 40.2 us (0.988)
  Pallas kernels: 39.9 us -> 39.4 us
    pallas_call x1, Pallas kernels: 37.6 us -> 37.1 us  [shards(): pl.pallas_call(step_kernel, out_shape=(jax.ShapeDtypeStruct((2, 16, SLAB,...]
where the time goes in v9:
time: 40.2 us; the launch traced here: 40 us
  Pallas kernels  39.4 us (98%)
  between operations  0.64 us (2%)
    pallas_call x1, Pallas kernels, shards(): pl.pallas_call(step_kernel, out_shape=(jax.ShapeDtypeStruct((2, 16, SLAB,...  37.1 us
    pallas_call x1, Pallas kernels, shards(): pl.pallas_call(finish_kernel, out_shape=(jax.ShapeDtypeStruct(weights.sha...  2.29 us

profile of v9, /device:TPU:1, one launch (start us, length us, event | category | flops | bytes accessed | tf_op | source)
XLA Modules:
  0.0 40.0 jit_solution(5005166804931350001)
XLA Ops:
  0.6 37.1 %step.1 = (bf16[2,16,80,128]{3,2,1,0:T(8,128)(2,1)}, f32[2,72,128]{2,1,0:T(8,128)}) custom-call(bf16[4,16,2,32,128]{4,3,2,1,0:T(8,128)(2,1)} %bitcast.2, bf16[4,16,2,32,128]{4,3,2,1,0:T(8,128)(2,1)} %bitcast.3, bf16[2,1152,128]{2,1,0:T(8,128)(2,1)} %w_hbm.1, f32[2,72,128]{2,1,0:T(8,128)} %master_hbm.3, f32[2,72,128]{2,1,0:T(8,128)} %first_hbm.3, ...), custom_call_target="tpu_custom_call" | custom-call | tf_op jit(solution)/shard_map/step/pallas_call | solution.py:400
  37.7 2.3 %finish.1 = (bf16[2,1152,128]{2,1,0:T(8,128)(2,1)}, f32[2,72,128]{2,1,0:T(8,128)}, f32[2,72,128]{2,1,0:T(8,128)}, f32[2,72,128]{2,1,0:T(8,128)}) custom-call(bf16[2,16,80,128]{3,2,1,0:T(8,128)(2,1)} %get-tuple-element.6.gathered_hbm, f32[2,72,128]{2,1,0:T(8,128)} %get-tuple-element.7.totals_hbm, f32[2,72,128]{2,1,0:T(8,128)} %master_hbm.3, ...), custom_call_target="tpu_custom_call" | custom-call | tf_op jit(solution)/shard_map/finish/pallas_call | solution.py:436

commit v10 on v9

--- a/solution.py
+++ b/solution.py
@@ -121,12 +121,12 @@
     loads = [
         pltpu.make_async_copy(src, dst, load_s.at[k])
         for k, (src, dst) in enumerate(
-            [(x_hbm, x_ref), (w_hbm, w_ref), (c_hbm, c_ref)]
+            [(w_hbm.at[0], w_ref.at[0]), (x_hbm, x_ref), (c_hbm, c_ref), (w_hbm.at[1], w_ref.at[1])]
             + [(ref.at[layer], state_ref.at[layer, k])
                for k, ref in enumerate((master_hbm, first_hbm, second_hbm)) for layer in range(2)]
         )
     ]
-    for copy in loads:
+    for copy in loads[:2]:
         copy.start()
     xy_order = [(kx, ky) for kx in (2, 1, 3, 0) for ky in (2, 1, 3, 0) if kx or ky]
     xy_steps = [(kx, ky) for kx in (0, 1, 3, 2) for ky in (0, 1, 3, 2) if kx or ky]
@@ -145,13 +145,9 @@
 
     own = y * 4 + x
 
-    def xy_copy(layer, shard):
-        other = 1 - core
-        kx, ky = lax.rem(shard % 4 + 4 - x, 4), lax.rem(shard // 4 + 4 - y, 4)
-        slot = other * 16 + kx * 4 + ky
-        target = (z_hi * 8 + shard // 4 * 2 + layer, z_lo * 4 + shard % 4)
-        copy = remote(xy_send.at[layer, shard], xy_recv.at[slot], xy_ss.at[layer, shard], xy_rs.at[slot], target)
-        return copy, slot > 0
+    def part_copy(kx, ky):
+        shard, slot = place(kx, ky), (1 - core) * 16 + kx * 4 + ky
+        return remote(xy_send.at[1, shard], xy_recv.at[slot], xy_ss.at[1, shard], xy_rs.at[slot], xy_peer(kx, ky, 1))
 
     def pair_copy(shard):
         return remote(grads.at[0, shard_rows(shard), :], pair_recv.at[shard], pair_ss.at[shard], pair_rs.at[shard], partner)
@@ -176,17 +172,17 @@
             else:
                 grads[0, shard_rows(shard), :] = both
 
-    def send_parts(layer, first, last):
-        for shard in range(first, last):
-            copy, remote_one = xy_copy(layer, shard)
-            pl.when(remote_one)(copy.start)
-
-    def round_parts(layer, first, last):
-        for shard in range(first, last):
-            xy_send[layer, shard, 0:ROWS, :] = grads[layer, shard_rows(shard), :].astype(BF16)
-
-    for copy in loads:
+    def send_parts():
+        for shard in range(16):
+            xy_send[1, shard, 0:ROWS, :] = grads[1, shard_rows(shard), :].astype(BF16)
+        for kx, ky in xy_order:
+            part_copy(kx, ky).start()
+        pl.when(core == 0)(part_copy(0, 0).start)
+
+    for copy in loads[:2]:
         copy.wait()
+    for copy in loads[2:]:
+        copy.start()
     pair_forward(w_ref, forward_w)
     shift_store(x_ref, x3, 0)
     for image in range(BATCH):
@@ -197,6 +193,9 @@
         slope[image] = sig + value * (1.0 - sig)
         if image < BATCH - 1:
             shift_store(x_ref, x3, image + 1)
+    for copy in loads[2:]:
+        copy.wait()
+    for image in range(BATCH):
         shift_store(c_ref, c3, image)
 
     pair_backward(w_ref, backward_w)
@@ -204,10 +203,9 @@
     for block in range(9):
         tap = 8 - block
         grads[1, tap * CHANS : (tap + 1) * CHANS, :] = out[:, block * CHANS : (block + 1) * CHANS]
-    round_parts(1, 0, 16)
 
     pl.semaphore_wait(barrier, len(peers))
-    send_parts(1, 0, 16)
+    send_parts()
 
     def held_copy(k, source_ref):
         return remote(source_ref, held, held_ss.at[k], held_rs, held_peer(k))
@@ -306,6 +304,27 @@
         for ky in (2, 1, 3):
             t_copy(ky).start()
 
+    @pl.when(core == 0)
+    def _():
+        part_copy(0, 0).wait_send()
+        for kx, ky in xy_steps:
+            pair_xy_copy(kx, ky).wait_send()
+
+    @pl.when(core == 1)
+    def _():
+        for k in range(16):
+            pair_copy(k).wait_send()
+
+    for kx, ky in xy_steps:
+        part_copy(kx, ky).wait_send()
+    for kz in z_order:
+        z_copy(kz, z).wait_send()
+
+    @pl.when(z_lo == y)
+    def _():
+        for k in range(1, 4):
+            held_copy(k, held).wait_send()
+
     def forward(steps):
         for kx, ky in steps:
             gat_copy(kx, ky, source(kx, ky)).wait_recv()
@@ -326,35 +345,19 @@
     puts[0].start()
     forward(xy_steps[3:])
     puts[1].start()
+    for kx, ky in xy_steps:
+        gat_copy(kx, ky, source(0, 0)).wait_send()
+
+    @pl.when(z_lo == y)
+    def _():
+        for k in range(1, 4):
+            t_copy(k).wait_send()
+
     remote(totals, totals_out.at[1 - core], tot_ss, tot_rs, partner).wait_recv()
     for kx, ky in xy_steps + [(0, 0)]:
         fwd_copy(1 - core, kx, ky).wait_recv()
     for k in range(16):
         fwd_copy(core, k // 4, k % 4).wait_send()
-        copy, remote_one = xy_copy(1, k)
-        pl.when(remote_one)(copy.wait_send)
-    for kx, ky in xy_steps:
-        gat_copy(kx, ky, source(0, 0)).wait_send()
-
-    @pl.when(core == 0)
-    def _():
-        for kx, ky in xy_steps:
-            pair_xy_copy(kx, ky).wait_send()
-
-    @pl.when(core == 1)
-    def _():
-        for k in range(16):
-            pair_copy(k).wait_send()
-
-    for kz in z_order:
-        z_copy(kz, z).wait_send()
-
-    @pl.when(z_lo == y)
-    def _():
-        for k in range(1, 4):
-            held_copy(k, held).wait_send()
-            t_copy(k).wait_send()
-
     tot.wait_send()
     for copy in puts:
         copy.wait()
@@ -425,7 +428,7 @@
             vmem((3, ROWS, CHANS), F32),
             vmem((ROWS, CHANS), F32),
             vmem((16, SLAB, CHANS), BF16),
-            dma((9,)),
+            dma((10,)),
             dma((16,)), dma((16,)), dma((2, 16)), dma((32,)), dma((8,)), dma((8,)), dma((4,)), dma,
             dma((4,)), dma, dma, dma, dma((16,)), dma((16,)), dma((16,)), dma((16,)), dma((2,)),
         ],

time: 40.2 us -> 40 us (level)
  no operation moved by 1% of the time
where the time goes in v10:
time: 40 us; the launch traced here: 39.9 us
  Pallas kernels  39.2 us (98%)
  between operations  0.64 us (2%)
    pallas_call x1, Pallas kernels, shards(): pl.pallas_call(step_kernel, out_shape=(jax.ShapeDtypeStruct((2, 16, SLAB,...  36.9 us
    pallas_call x1, Pallas kernels, shards(): pl.pallas_call(finish_kernel, out_shape=(jax.ShapeDtypeStruct(weights.sha...  2.29 us

profile of v10, /device:TPU:1, one launch (start us, length us, event | category | flops | bytes accessed | tf_op | source)
XLA Modules:
  0.0 39.9 jit_solution(11173426184237332658)
XLA Ops:
  0.6 36.9 %step.1 = (bf16[2,16,80,128]{3,2,1,0:T(8,128)(2,1)}, f32[2,72,128]{2,1,0:T(8,128)}) custom-call(bf16[4,16,2,32,128]{4,3,2,1,0:T(8,128)(2,1)} %bitcast.2, bf16[4,16,2,32,128]{4,3,2,1,0:T(8,128)(2,1)} %bitcast.3, bf16[2,1152,128]{2,1,0:T(8,128)(2,1)} %w_hbm.1, f32[2,72,128]{2,1,0:T(8,128)} %master_hbm.3, f32[2,72,128]{2,1,0:T(8,128)} %first_hbm.3, ...), custom_call_target="tpu_custom_call" | custom-call | tf_op jit(solution)/shard_map/step/pallas_call | solution.py:403
  37.6 2.3 %finish.1 = (bf16[2,1152,128]{2,1,0:T(8,128)(2,1)}, f32[2,72,128]{2,1,0:T(8,128)}, f32[2,72,128]{2,1,0:T(8,128)}, f32[2,72,128]{2,1,0:T(8,128)}) custom-call(bf16[2,16,80,128]{3,2,1,0:T(8,128)(2,1)} %get-tuple-element.6.gathered_hbm, f32[2,72,128]{2,1,0:T(8,128)} %get-tuple-element.7.totals_hbm, f32[2,72,128]{2,1,0:T(8,128)} %master_hbm.3, ...), custom_call_target="tpu_custom_call" | custom-call | tf_op jit(solution)/shard_map/finish/pallas_call | solution.py:439

commit v11 on v10

--- a/solution.py
+++ b/solution.py
@@ -156,21 +156,20 @@
         for shard in range(first, last):
             pair_copy(shard).start()
 
-    def pair_xy_copy(kx, ky):
-        slot, shard = kx * 4 + ky, place(kx, ky)
-        target = xy_peer(kx, ky)
-        return remote(xy_send.at[0, shard], xy_recv.at[slot], xy_ss.at[0, shard], xy_rs.at[slot], target)
+    def pair_xy_copy(shard):
+        slot = lax.rem(shard % 4 + 4 - x, 4) * 4 + lax.rem(shard // 4 + 4 - y, 4)
+        target = (z_hi * 8 + shard // 4 * 2 + core, z_lo * 4 + shard % 4)
+        copy = remote(xy_send.at[0, shard], xy_recv.at[slot], xy_ss.at[0, shard], xy_rs.at[slot], target)
+        return copy, slot > 0
 
     def sum_pair():
-        for kx, ky in xy_order + [(0, 0)]:
-            shard = place(kx, ky)
+        for shard in range(16):
             pair_copy(shard).wait_recv()
             both = grads[0, shard_rows(shard), :] + pair_recv[shard]
-            if kx or ky:
-                xy_send[0, shard, 0:ROWS, :] = both.astype(BF16)
-                pair_xy_copy(kx, ky).start()
-            else:
-                grads[0, shard_rows(shard), :] = both
+            grads[0, shard_rows(shard), :] = both
+            xy_send[0, shard, 0:ROWS, :] = both.astype(BF16)
+            copy, away = pair_xy_copy(shard)
+            pl.when(away)(copy.start)
 
     def send_parts():
         for shard in range(16):
@@ -307,8 +306,9 @@
     @pl.when(core == 0)
     def _():
         part_copy(0, 0).wait_send()
-        for kx, ky in xy_steps:
-            pair_xy_copy(kx, ky).wait_send()
+        for shard in range(16):
+            copy, away = pair_xy_copy(shard)
+            pl.when(away)(copy.wait_send)
 
     @pl.when(core == 1)
     def _():

time: 40 us -> 39.9 us (level)
  no operation moved by 1% of the time
where the time goes in v11:
time: 39.9 us; the launch traced here: 39.8 us
  Pallas kernels  39.1 us (98%)
  between operations  0.64 us (2%)
    pallas_call x1, Pallas kernels, shards(): pl.pallas_call(step_kernel, out_shape=(jax.ShapeDtypeStruct((2, 16, SLAB,...  36.8 us
    pallas_call x1, Pallas kernels, shards(): pl.pallas_call(finish_kernel, out_shape=(jax.ShapeDtypeStruct(weights.sha...  2.29 us

profile of v11, /device:TPU:1, one launch (start us, length us, event | category | flops | bytes accessed | tf_op | source)
XLA Modules:
  0.0 39.8 jit_solution(4693625702490272707)
XLA Ops:
  0.6 36.8 %step.1 = (bf16[2,16,80,128]{3,2,1,0:T(8,128)(2,1)}, f32[2,72,128]{2,1,0:T(8,128)}) custom-call(bf16[4,16,2,32,128]{4,3,2,1,0:T(8,128)(2,1)} %bitcast.2, bf16[4,16,2,32,128]{4,3,2,1,0:T(8,128)(2,1)} %bitcast.3, bf16[2,1152,128]{2,1,0:T(8,128)(2,1)} %w_hbm.1, f32[2,72,128]{2,1,0:T(8,128)} %master_hbm.3, f32[2,72,128]{2,1,0:T(8,128)} %first_hbm.3, ...), custom_call_target="tpu_custom_call" | custom-call | tf_op jit(solution)/shard_map/step/pallas_call | solution.py:403
  37.5 2.3 %finish.1 = (bf16[2,1152,128]{2,1,0:T(8,128)(2,1)}, f32[2,72,128]{2,1,0:T(8,128)}, f32[2,72,128]{2,1,0:T(8,128)}, f32[2,72,128]{2,1,0:T(8,128)}) custom-call(bf16[2,16,80,128]{3,2,1,0:T(8,128)(2,1)} %get-tuple-element.6.gathered_hbm, f32[2,72,128]{2,1,0:T(8,128)} %get-tuple-element.7.totals_hbm, f32[2,72,128]{2,1,0:T(8,128)} %master_hbm.3, ...), custom_call_target="tpu_custom_call" | custom-call | tf_op jit(solution)/shard_map/finish/pallas_call | solution.py:439

commit v12 on v11

--- a/solution.py
+++ b/solution.py
@@ -231,11 +231,17 @@
     def _():
         send_pair(0, 8)
 
-    first_layer(5, 9)
+    first_layer(5, 7)
 
     @pl.when(core == 1)
     def _():
-        send_pair(8, 16)
+        send_pair(8, 12)
+
+    first_layer(7, 9)
+
+    @pl.when(core == 1)
+    def _():
+        send_pair(12, 16)
 
     @pl.when(core == 0)
     def _():

time: 39.9 us -> 40.6 us (1.018)
  Pallas kernels: 39.1 us -> 39.8 us
    pallas_call x1, Pallas kernels: 36.8 us -> 37.5 us  [shards(): pl.pallas_call(step_kernel, out_shape=(jax.ShapeDtypeStruct((2, 16, SLAB,...]
where the time goes in v12:
time: 40.6 us; the launch traced here: 40.5 us
  Pallas kernels  39.8 us (98%)
  between operations  0.64 us (2%)
    pallas_call x1, Pallas kernels, shards(): pl.pallas_call(step_kernel, out_shape=(jax.ShapeDtypeStruct((2, 16, SLAB,...  37.5 us
    pallas_call x1, Pallas kernels, shards(): pl.pallas_call(finish_kernel, out_shape=(jax.ShapeDtypeStruct(weights.sha...  2.29 us

profile of v12, /device:TPU:1, one launch (start us, length us, event | category | flops | bytes accessed | tf_op | source)
XLA Modules:
  0.0 40.5 jit_solution(18195405201295406585)
XLA Ops:
  0.6 37.5 %step.1 = (bf16[2,16,80,128]{3,2,1,0:T(8,128)(2,1)}, f32[2,72,128]{2,1,0:T(8,128)}) custom-call(bf16[4,16,2,32,128]{4,3,2,1,0:T(8,128)(2,1)} %bitcast.2, bf16[4,16,2,32,128]{4,3,2,1,0:T(8,128)(2,1)} %bitcast.3, bf16[2,1152,128]{2,1,0:T(8,128)(2,1)} %w_hbm.1, f32[2,72,128]{2,1,0:T(8,128)} %master_hbm.3, f32[2,72,128]{2,1,0:T(8,128)} %first_hbm.3, ...), custom_call_target="tpu_custom_call" | custom-call | tf_op jit(solution)/shard_map/step/pallas_call | solution.py:409
  38.2 2.3 %finish.1 = (bf16[2,1152,128]{2,1,0:T(8,128)(2,1)}, f32[2,72,128]{2,1,0:T(8,128)}, f32[2,72,128]{2,1,0:T(8,128)}, f32[2,72,128]{2,1,0:T(8,128)}) custom-call(bf16[2,16,80,128]{3,2,1,0:T(8,128)(2,1)} %get-tuple-element.6.gathered_hbm, f32[2,72,128]{2,1,0:T(8,128)} %get-tuple-element.7.totals_hbm, f32[2,72,128]{2,1,0:T(8,128)} %master_hbm.3, ...), custom_call_target="tpu_custom_call" | custom-call | tf_op jit(solution)/shard_map/finish/pallas_call | solution.py:445

commit v13 on v11

--- a/solution.py
+++ b/solution.py
@@ -225,17 +225,17 @@
             block = out[:, (tap - first) * CHANS : (tap + 1 - first) * CHANS]
             grads[0, tap * CHANS : (tap + 1) * CHANS, :] = block.T
 
-    first_layer(0, 5)
+    first_layer(0, 6)
 
     @pl.when(core == 1)
     def _():
-        send_pair(0, 8)
-
-    first_layer(5, 9)
+        send_pair(0, 10)
+
+    first_layer(6, 9)
 
     @pl.when(core == 1)
     def _():
-        send_pair(8, 16)
+        send_pair(10, 16)
 
     @pl.when(core == 0)
     def _():

time: 39.9 us -> 40.4 us (1.013)
  Pallas kernels: 39.1 us -> 39.6 us
    pallas_call x1, Pallas kernels: 36.8 us -> 37.3 us  [shards(): pl.pallas_call(step_kernel, out_shape=(jax.ShapeDtypeStruct((2, 16, SLAB,...]
where the time goes in v13:
time: 40.4 us; the launch traced here: 40.2 us
  Pallas kernels  39.6 us (98%)
  between operations  0.64 us (2%)
    pallas_call x1, Pallas kernels, shards(): pl.pallas_call(step_kernel, out_shape=(jax.ShapeDtypeStruct((2, 16, SLAB,...  37.3 us
    pallas_call x1, Pallas kernels, shards(): pl.pallas_call(finish_kernel, out_shape=(jax.ShapeDtypeStruct(weights.sha...  2.29 us

profile of v13, /device:TPU:1, one launch (start us, length us, event | category | flops | bytes accessed | tf_op | source)
XLA Modules:
  0.0 40.2 jit_solution(2588842024536087051)
XLA Ops:
  0.6 37.3 %step.1 = (bf16[2,16,80,128]{3,2,1,0:T(8,128)(2,1)}, f32[2,72,128]{2,1,0:T(8,128)}) custom-call(bf16[4,16,2,32,128]{4,3,2,1,0:T(8,128)(2,1)} %bitcast.2, bf16[4,16,2,32,128]{4,3,2,1,0:T(8,128)(2,1)} %bitcast.3, bf16[2,1152,128]{2,1,0:T(8,128)(2,1)} %w_hbm.1, f32[2,72,128]{2,1,0:T(8,128)} %master_hbm.3, f32[2,72,128]{2,1,0:T(8,128)} %first_hbm.3, ...), custom_call_target="tpu_custom_call" | custom-call | tf_op jit(solution)/shard_map/step/pallas_call | solution.py:403
  38.0 2.3 %finish.1 = (bf16[2,1152,128]{2,1,0:T(8,128)(2,1)}, f32[2,72,128]{2,1,0:T(8,128)}, f32[2,72,128]{2,1,0:T(8,128)}, f32[2,72,128]{2,1,0:T(8,128)}) custom-call(bf16[2,16,80,128]{3,2,1,0:T(8,128)(2,1)} %get-tuple-element.6.gathered_hbm, f32[2,72,128]{2,1,0:T(8,128)} %get-tuple-element.7.totals_hbm, f32[2,72,128]{2,1,0:T(8,128)} %master_hbm.3, ...), custom_call_target="tpu_custom_call" | custom-call | tf_op jit(solution)/shard_map/finish/pallas_call | solution.py:439
